TPU v7x, 32 devices: a whole 2x2x4 slice. The times are simulated.
32 devices in a mesh: shard: 16 (over z, y, core), seq: 2 (over x).
Axes of the slice: x: 2, y: 2, z: 4, core: 2. Of those that a mesh axis runs over, the one named last changes fastest.
Arguments:
- tokens: bfloat16 [32, 1024, 1024], P('shard', 'seq'), may hold values from -6 to 6
- condition: bfloat16 [32, 1024], P('shard'), may hold values from -6 to 6
- cotangent: bfloat16 [32, 1024, 1024], P('shard', 'seq'), may hold values from -6 to 6
- ada_weight: bfloat16 [1024, 6144], P('shard'), may hold values from -0.1875 to 0.1875
- ada_bias: bfloat16 [6144], P('shard'), may hold values from -4 to 4
- qkv_weight: bfloat16 [1024, 3072], P('shard'), may hold values from -0.1875 to 0.1875
- qv_bias: bfloat16 [2048], P('shard'), may hold values from -3 to 3
- proj_weight: bfloat16 [1024, 1024], P('shard'), may hold values from -0.75 to 0.75
- proj_bias: bfloat16 [1024], P('shard'), may hold values from -3 to 3
- up_weight: bfloat16 [1024, 4096], P('shard'), may hold values from -0.1875 to 0.1875
- up_bias: bfloat16 [4096], P('shard'), may hold values from -3 to 3
- down_weight: bfloat16 [4096, 1024], P('shard'), may hold values from -0.09375 to 0.09375
- down_bias: bfloat16 [1024], P('shard'), may hold values from -3 to 3
Outputs:
- result: bfloat16 [32, 1024, 1024], P('shard', 'seq')
- grad_tokens: float32 [32, 1024, 1024], P('shard', 'seq')
- grad_condition: float32 [32, 1024], P('shard')
- grad_ada_weight: float32 [1024, 6144], P('shard')
- grad_ada_bias: float32 [6144], P('shard')
- grad_qkv_weight: float32 [1024, 3072], P('shard')
- grad_qv_bias: float32 [2048], P('shard')
- grad_proj_weight: float32 [1024, 1024], P('shard')
- grad_proj_bias: float32 [1024], P('shard')
- grad_up_weight: float32 [1024, 4096], P('shard')
- grad_up_bias: float32 [4096], P('shard')
- grad_down_weight: float32 [4096, 1024], P('shard')
- grad_down_bias: float32 [1024], P('shard')
All inputs are finite; a program needn't handle non-finite values.
Results may differ from a plain program's by a relative error of at most 0.02.
The roundings to bfloat16 on the way count: a program that leaves them out, or rounds other values in their place, can miss the bound.
Values may be sent and summed in bfloat16 or wider, within the bound.
A program may use at most 320 MiB of HBM per device.

v0:
```python
import math

import jax
import jax.numpy as jnp
from jax import lax
from jax.sharding import PartitionSpec as P

HD = 64


epsilon = 1e-06


def as_sent(x):
    return jax.tree.map(lambda a: a.astype(jnp.bfloat16) if a.dtype == jnp.float32 else a, x)


def modulate(residual, shift, scale):
    average = jnp.mean(residual, -1, keepdims=True)
    centred = residual - average
    spread = jnp.mean(centred * centred, -1, keepdims=True)
    return centred * lax.rsqrt(spread + epsilon) * (1.0 + scale[:, None, :]) + shift[:, None, :]


def gelu_tanh(values):
    return jax.nn.gelu(values, approximate=True)


def heads_of(matrix):
    return matrix.reshape(matrix.shape[0], matrix.shape[1] // HD, HD)


def attend_latent(stacked):
    length = stacked.shape[0]
    block_rows = min(512, length)
    factor = 1.0 / math.sqrt(HD)
    query_rows = heads_of(stacked[:, 0])
    key_rows = heads_of(stacked[:, 1])
    value_rows = heads_of(stacked[:, 2])
    outputs = []
    totals = []
    for offset in range(0, length, block_rows):
        scores = (
            jnp.einsum(
                "qhd,khd->hqk",
                query_rows[offset : offset + block_rows],
                key_rows,
                preferred_element_type=jnp.float32,
            )
            * factor
        )
        top_score = jnp.max(scores, axis=-1, keepdims=True)
        shifted = jnp.exp(scores - top_score)
        denominator = jnp.sum(shifted, axis=-1, keepdims=True)
        attn_probs = (shifted / denominator).astype(jnp.bfloat16)
        combined = jnp.einsum(
            "hqk,khd->qhd", attn_probs, value_rows, preferred_element_type=jnp.float32
        )
        outputs.append(combined.reshape(block_rows, -1).astype(jnp.bfloat16))
        totals.append((top_score + jnp.log(denominator))[:, :, 0])
    return (jnp.concatenate(outputs, 0), jnp.concatenate(totals, 1))


def attend_back(pieces):
    stacked, grad_out, log_totals = pieces
    length = stacked.shape[0]
    block_rows = min(512, length)
    factor = 1.0 / math.sqrt(HD)
    query_rows = heads_of(stacked[:, 0])
    key_rows = heads_of(stacked[:, 1])
    value_rows = heads_of(stacked[:, 2])
    grad_heads = heads_of(grad_out)
    grad_keys = jnp.zeros(key_rows.shape, jnp.float32)
    grad_values = jnp.zeros(value_rows.shape, jnp.float32)
    query_grads = []
    for offset in range(0, length, block_rows):
        query_block = query_rows[offset : offset + block_rows]
        grad_block = grad_heads[offset : offset + block_rows]
        scores = (
            jnp.einsum("qhd,khd->hqk", query_block, key_rows, preferred_element_type=jnp.float32)
            * factor
        )
        attn_probs = jnp.exp(scores - log_totals[:, offset : offset + block_rows, None])
        grad_probs = jnp.einsum(
            "qhd,khd->hqk", grad_block, value_rows, preferred_element_type=jnp.float32
        )
        row_delta = jnp.sum(attn_probs * grad_probs, axis=-1, keepdims=True)
        grad_scores = (attn_probs * (grad_probs - row_delta)).astype(jnp.bfloat16)
        grad_query = (
            jnp.einsum("hqk,khd->qhd", grad_scores, key_rows, preferred_element_type=jnp.float32)
            * factor
        )
        query_grads.append(grad_query.reshape(block_rows, -1).astype(jnp.bfloat16))
        grad_keys = (
            grad_keys
            + jnp.einsum(
                "hqk,qhd->khd", grad_scores, query_block, preferred_element_type=jnp.float32
            )
            * factor
        )
        grad_values = grad_values + jnp.einsum(
            "hqk,qhd->khd",
            attn_probs.astype(jnp.bfloat16),
            grad_block,
            preferred_element_type=jnp.float32,
        )
    grad_query_all = jnp.concatenate(query_grads, 0)
    grad_key_all = grad_keys.reshape(length, -1).astype(jnp.bfloat16)
    grad_value_all = grad_values.reshape(length, -1).astype(jnp.bfloat16)
    return jnp.stack([grad_query_all, grad_key_all, grad_value_all], axis=1)


def shards(
    tokens,
    condition,
    cotangent,
    ada_weight,
    ada_bias,
    qkv_weight,
    qv_bias,
    proj_weight,
    proj_bias,
    up_weight,
    up_bias,
    down_weight,
    down_bias,
):
    gathered = (
        lax.all_gather(ada_weight, "shard", axis=0, tiled=True),
        lax.all_gather(ada_bias, "shard", axis=0, tiled=True),
        lax.all_gather(qkv_weight, "shard", axis=0, tiled=True),
        lax.all_gather(qv_bias, "shard", axis=0, tiled=True),
        lax.all_gather(proj_weight, "shard", axis=0, tiled=True),
        lax.all_gather(proj_bias, "shard", axis=0, tiled=True),
        lax.all_gather(up_weight, "shard", axis=0, tiled=True),
        lax.all_gather(up_bias, "shard", axis=0, tiled=True),
        lax.all_gather(down_weight, "shard", axis=0, tiled=True),
        lax.all_gather(down_bias, "shard", axis=0, tiled=True),
    )
    w_ada, b_ada, w_qkv, b_qv, w_proj, b_proj, w_up, b_up, w_down, b_down = gathered
    latents, local_rows, model_width = tokens.shape
    cond_float = condition.astype(jnp.float32)
    cond_act = jax.nn.silu(cond_float).astype(jnp.bfloat16)
    modulation = jnp.dot(cond_act, w_ada, preferred_element_type=jnp.float32) + b_ada.astype(
        jnp.float32
    )
    shift_one, scale_one, gate_one, shift_two, scale_two, gate_two = jnp.split(
        modulation, 6, axis=1
    )
    residual = tokens.astype(jnp.float32)
    normed_one = modulate(residual, shift_one, scale_one).astype(jnp.bfloat16)
    project = jnp.einsum("btd,de->bte", normed_one, w_qkv, preferred_element_type=jnp.float32)
    bias_qv = b_qv.astype(jnp.float32)
    qkv_biases = jnp.stack(
        [bias_qv[:model_width], jnp.zeros((model_width,), jnp.float32), bias_qv[model_width:]]
    )
    stacked = (project.reshape(latents, local_rows, 3, model_width) + qkv_biases).astype(
        jnp.bfloat16
    )
    by_heads = lax.all_to_all(stacked, "seq", split_axis=3, concat_axis=1, tiled=True)
    attn_heads, log_totals = lax.map(attend_latent, by_heads)
    attended = jax.tree.map(
        lambda part, own: part.astype(own.dtype),
        lax.all_to_all(as_sent(attn_heads), "seq", split_axis=1, concat_axis=2, tiled=True),
        attn_heads,
    )
    branch = jnp.einsum(
        "bte,ed->btd", attended, w_proj, preferred_element_type=jnp.float32
    ) + b_proj.astype(jnp.float32)
    middle = residual + gate_one[:, None, :] * branch
    normed_two = modulate(middle, shift_two, scale_two).astype(jnp.bfloat16)
    hidden = jnp.einsum(
        "btd,df->btf", normed_two, w_up, preferred_element_type=jnp.float32
    ) + b_up.astype(jnp.float32)
    active = gelu_tanh(hidden).astype(jnp.bfloat16)
    output = jnp.einsum(
        "btf,fd->btd", active, w_down, preferred_element_type=jnp.float32
    ) + b_down.astype(jnp.float32)
    result = (middle + gate_two[:, None, :] * output).astype(jnp.bfloat16)
    again = (
        lax.all_gather(ada_weight, "shard", axis=0, tiled=True),
        lax.all_gather(ada_bias, "shard", axis=0, tiled=True),
        lax.all_gather(qkv_weight, "shard", axis=0, tiled=True),
        lax.all_gather(qv_bias, "shard", axis=0, tiled=True),
        lax.all_gather(proj_weight, "shard", axis=0, tiled=True),
        lax.all_gather(proj_bias, "shard", axis=0, tiled=True),
        lax.all_gather(up_weight, "shard", axis=0, tiled=True),
        lax.all_gather(up_bias, "shard", axis=0, tiled=True),
        lax.all_gather(down_weight, "shard", axis=0, tiled=True),
        lax.all_gather(down_bias, "shard", axis=0, tiled=True),
    )
    w_ada, b_ada, w_qkv, b_qv, w_proj, b_proj, w_up, b_up, w_down, b_down = again
    grad_result = cotangent.astype(jnp.float32)
    grad_output = (gate_two[:, None, :] * grad_result).astype(jnp.bfloat16)
    grad_gate_two = jnp.sum(grad_result * output, axis=1)
    grad_down_weight = jnp.einsum(
        "btf,btd->fd", active, grad_output, preferred_element_type=jnp.float32
    )
    grad_down_bias = jnp.sum(grad_output, axis=(0, 1), dtype=jnp.float32)
    grad_active = jnp.einsum("btd,fd->btf", grad_output, w_down, preferred_element_type=jnp.float32)
    unused, gelu_back = jax.vjp(gelu_tanh, hidden)
    grad_hidden = gelu_back(grad_active)[0].astype(jnp.bfloat16)
    grad_up_weight = jnp.einsum(
        "btd,btf->df", normed_two, grad_hidden, preferred_element_type=jnp.float32
    )
    grad_up_bias = jnp.sum(grad_hidden, axis=(0, 1), dtype=jnp.float32)
    grad_normed_two = jnp.einsum(
        "btf,df->btd", grad_hidden, w_up, preferred_element_type=jnp.float32
    )
    unused, norm_back_two = jax.vjp(modulate, middle, shift_two, scale_two)
    grad_middle, grad_shift_two, grad_scale_two = norm_back_two(grad_normed_two)
    grad_middle = grad_middle + grad_result
    grad_branch = (gate_one[:, None, :] * grad_middle).astype(jnp.bfloat16)
    grad_gate_one = jnp.sum(grad_middle * branch, axis=1)
    grad_proj_weight = jnp.einsum(
        "bte,btd->ed", attended, grad_branch, preferred_element_type=jnp.float32
    )
    grad_proj_bias = jnp.sum(grad_branch, axis=(0, 1), dtype=jnp.float32)
    grad_attended = jnp.einsum(
        "btd,ed->bte", grad_branch, w_proj, preferred_element_type=jnp.float32
    ).astype(jnp.bfloat16)
    grad_by_heads = lax.all_to_all(grad_attended, "seq", split_axis=2, concat_axis=1, tiled=True)
    grad_stacked = lax.map(attend_back, (by_heads, grad_by_heads, log_totals))
    grad_qkv = jax.tree.map(
        lambda part, own: part.astype(own.dtype),
        lax.all_to_all(as_sent(grad_stacked), "seq", split_axis=1, concat_axis=3, tiled=True),
        grad_stacked,
    )
    grad_flat = grad_qkv.reshape(latents, local_rows, 3 * model_width)
    grad_qkv_weight = jnp.einsum(
        "btd,bte->de", normed_one, grad_flat, preferred_element_type=jnp.float32
    )
    column_sums = jnp.sum(grad_qkv, axis=(0, 1), dtype=jnp.float32)
    grad_qv_bias = jnp.concatenate([column_sums[0], column_sums[2]])
    grad_normed_one = jnp.einsum(
        "bte,de->btd", grad_flat, w_qkv, preferred_element_type=jnp.float32
    )
    unused, norm_back_one = jax.vjp(modulate, residual, shift_one, scale_one)
    grad_input, grad_shift_one, grad_scale_one = norm_back_one(grad_normed_one)
    grad_tokens = grad_input + grad_middle
    grad_modulation = jnp.concatenate(
        [
            grad_shift_one,
            grad_scale_one,
            grad_gate_one,
            grad_shift_two,
            grad_scale_two,
            grad_gate_two,
        ],
        axis=1,
    )
    grad_modulation = lax.psum(grad_modulation.astype(jnp.bfloat16), "seq")
    grad_ada_weight = jnp.einsum(
        "bd,be->de", cond_act, grad_modulation, preferred_element_type=jnp.float32
    )
    grad_ada_bias = jnp.sum(grad_modulation, axis=0, dtype=jnp.float32)
    grad_cond_act = jnp.einsum(
        "be,de->bd", grad_modulation, w_ada, preferred_element_type=jnp.float32
    )
    unused, silu_back = jax.vjp(jax.nn.silu, cond_float)
    grad_condition = silu_back(grad_cond_act)[0]
    owned_rows = (
        lax.psum_scatter(
            grad_ada_weight.astype(jnp.bfloat16), "shard", scatter_dimension=0, tiled=True
        ).astype(jnp.float32),
        lax.psum_scatter(
            grad_ada_bias.astype(jnp.bfloat16), "shard", scatter_dimension=0, tiled=True
        ).astype(jnp.float32),
        lax.psum_scatter(
            grad_qkv_weight.astype(jnp.bfloat16), "shard", scatter_dimension=0, tiled=True
        ).astype(jnp.float32),
        lax.psum_scatter(
            grad_qv_bias.astype(jnp.bfloat16), "shard", scatter_dimension=0, tiled=True
        ).astype(jnp.float32),
        lax.psum_scatter(
            grad_proj_weight.astype(jnp.bfloat16), "shard", scatter_dimension=0, tiled=True
        ).astype(jnp.float32),
        lax.psum_scatter(
            grad_proj_bias.astype(jnp.bfloat16), "shard", scatter_dimension=0, tiled=True
        ).astype(jnp.float32),
        lax.psum_scatter(
            grad_up_weight.astype(jnp.bfloat16), "shard", scatter_dimension=0, tiled=True
        ).astype(jnp.float32),
        lax.psum_scatter(
            grad_up_bias.astype(jnp.bfloat16), "shard", scatter_dimension=0, tiled=True
        ).astype(jnp.float32),
        lax.psum_scatter(
            grad_down_weight.astype(jnp.bfloat16), "shard", scatter_dimension=0, tiled=True
        ).astype(jnp.float32),
        lax.psum_scatter(
            grad_down_bias.astype(jnp.bfloat16), "shard", scatter_dimension=0, tiled=True
        ).astype(jnp.float32),
    )
    summed_rest = (
        lax.psum(owned_rows[2].astype(jnp.bfloat16), "seq").astype(jnp.float32),
        lax.psum(owned_rows[3].astype(jnp.bfloat16), "seq").astype(jnp.float32),
        lax.psum(owned_rows[4].astype(jnp.bfloat16), "seq").astype(jnp.float32),
        lax.psum(owned_rows[5].astype(jnp.bfloat16), "seq").astype(jnp.float32),
        lax.psum(owned_rows[6].astype(jnp.bfloat16), "seq").astype(jnp.float32),
        lax.psum(owned_rows[7].astype(jnp.bfloat16), "seq").astype(jnp.float32),
        lax.psum(owned_rows[8].astype(jnp.bfloat16), "seq").astype(jnp.float32),
        lax.psum(owned_rows[9].astype(jnp.bfloat16), "seq").astype(jnp.float32),
    )
    finished = (owned_rows[0], owned_rows[1]) + tuple(summed_rest)
    return (
        result,
        grad_tokens,
        grad_condition,
        finished[0],
        finished[1],
        finished[2],
        finished[3],
        finished[4],
        finished[5],
        finished[6],
        finished[7],
        finished[8],
        finished[9],
    )


def solution(mesh):
    in_specs = (
        P("shard", "seq", None),
        P("shard", None),
        P("shard", "seq", None),
        P("shard", None),
        P("shard"),
        P("shard", None),
        P("shard"),
        P("shard", None),
        P("shard"),
        P("shard", None),
        P("shard"),
        P("shard", None),
        P("shard"),
    )
    out_specs = (
        P("shard", "seq", None),
        P("shard", "seq", None),
        P("shard", None),
        P("shard", None),
        P("shard"),
        P("shard", None),
        P("shard"),
        P("shard", None),
        P("shard"),
        P("shard", None),
        P("shard"),
        P("shard", None),
        P("shard"),
    )
    return jax.shard_map(shards, mesh=mesh, in_specs=in_specs, out_specs=out_specs, check_vma=False)
```

profile of v0, /device:TPU:0, one launch (start us, length us, event | category | flops | bytes accessed | tf_op | source)
XLA Modules:
  0.0 1220.8 jit_solution(15536099714147260130)
XLA Ops:
  10.7 23.6 %all-gather = bf16[16,1,384]{2,1,0:T(2,128)(2,1)S(1)} all-gather(bf16[1,1,384]{2,1,0:T(2,128)(2,1)S(1)} %reshape.175), channel_id=1, replica_groups=mesh['shard'=16,'seq'=2] {'shard'}, dimensions={0}, use_global_device_ids=true | all-gather | bytes 13056 | tf_op jit(solution)/shard_map/all_gather | solution.py:130
  34.3 17.8 %all-gather.1 = bf16[16,1,128]{2,1,0:T(2,128)(2,1)S(1)} all-gather(bf16[1,1,128]{2,1,0:T(2,128)(2,1)} %bitcast.298), channel_id=1, replica_groups=mesh['shard'=16,'seq'=2] {'shard'}, dimensions={0}, use_global_device_ids=true | all-gather | bytes 4352 | tf_op jit(solution)/shard_map/all_gather | solution.py:132
  57.3 56.6 %all-gather.9.cloned.1.call-done = bf16[1024,6144]{1,0:T(8,128)(2,1)} async-done(((bf16[64,6144]{1,0:T(8,128)(2,1)}), bf16[1024,6144]{1,0:T(8,128)(2,1)}) %all-gather.9.cloned.1.call-update) | async-done | bytes 12582928 | tf_op jit(solution)/shard_map/all_gather | solution.py:129
  121.0 55.2 %all-gather.11.cloned.1.call-done = bf16[1024,3072]{1,0:T(8,128)(2,1)} async-done(((bf16[64,3072]{1,0:T(8,128)(2,1)}), bf16[1024,3072]{1,0:T(8,128)(2,1)}) %all-gather.11.cloned.1.call-update) | async-done | bytes 6291472 | tf_op jit(solution)/shard_map/all_gather | solution.py:131
  216.8 69.9 %all-to-all-done = bf16[2,512,3,1024]{1,0,2,3:T(2,128)(2,1)} async-done(((bf16[2,512,3,1024]{1,0,2,3:T(2,128)(2,1)}), bf16[2,512,3,1024]{1,0,2,3:T(2,128)(2,1)}, u32[]{:S(2)}, u32[]{:S(2)}) %all-to-all-start) | async-done | bytes 6291488 | tf_op jit(solution)/shard_map/all_to_all | solution.py:160
  310.9 74.1 %while.22 = (s32[]{:T(128)}, bf16[2,1024,512]{1,2,0:T(8,128)(2,1)S(1)}, f32[2,8,1024]{2,1,0:T(8,128)S(1)}, bf16[2,1024,3,512]{1,3,2,0:T(8,128)(2,1)}, s32[]{:T(128)}) while((s32[]{:T(128)}, bf16[2,1024,512]{1,2,0:T(8,128)(2,1)S(1)}, f32[2,8,1024]{2,1,0:T(8,128)S(1)}, bf16[2,1024,3,512]{1,3,2,0:T(8,128)(2,1)}, s32[]{:T(128)}) %tuple.104), condition=%wide.region_7.8_spmd, body=%wide.region_2.7_spmd.sunk | while | flops 2225602560 | bytes 121962560 | solution.py:161
  395.9 30.9 %all-reduce.8 = (bf16[1024]{0:T(1024)(128)(2,1)S(1)}, bf16[1024]{0:T(1024)(128)(2,1)}) all-reduce(bf16[1024]{0:T(1024)(128)(2,1)S(1)} %dynamic-update-slice, bf16[1024]{0:T(1024)(128)(2,1)S(1)} %dynamic-update-slice.1), channel_id=1, replica_groups=mesh['shard'=16,'seq'=2] {'shard'}, use_global_device_ids=true, to_apply=%add | all-reduce | flops 2048 | bytes 8192
  426.8 17.4 %all-gather.2 = bf16[16,1,256]{2,1,0:T(2,128)(2,1)S(1)} all-gather(bf16[1,1,256]{2,1,0:T(2,128)(2,1)S(1)} %reshape.179), channel_id=1, replica_groups=mesh['shard'=16,'seq'=2] {'shard'}, dimensions={0}, use_global_device_ids=true | all-gather | bytes 8704 | tf_op jit(solution)/shard_map/all_gather | solution.py:136
  463.2 16.1 %fusion.40 = f32[2,512,4096]{2,1,0:T(8,128)} fusion(bf16[1024,4096]{1,0:T(8,128)(2,1)} %all-gather.15.cloned.1.call-done, f32[2,512,1024]{2,1,0:T(8,128)} %copy-done.13, f32[2,1024]{1,0:T(2,128)S(1)} %copy-done.45, f32[2,1024]{1,0:T(2,128)S(1)} %copy-done.33, f32[2,512]{1,0:T(2,128)S(1)} %fusion.83, f32[2,512]{1,0:T(2,128)S(1)} %broadcast_multiply_fusion), kind=kOutput, calls=%fused_computation.71 | convolution fusion | flops 8595177472 | bytes 29384704 | tf_op jit(solution)/shard_map/btd,df->btf/dot_general | solution.py:172
  479.4 24.6 %fusion.99 = (bf16[4096]{0:T(1024)(128)(2,1)}, bf16[2,512,4096]{2,1,0:T(8,128)(2,1)}) fusion(f32[2,512,4096]{2,1,0:T(8,128)} %fusion.40, f32[4096]{0:T(1024)S(1)} %bitcast.293, bf16[4096,1024]{1,0:T(8,128)(2,1)} %all-gather.17.cloned.1.call-done, bf16[2,512,1024]{2,1,0:T(8,128)(2,1)S(1)} %copy-done.17, f32[2,1024]{1,0:T(2,128)S(1)} %copy-done.28), kind=kOutput, calls=%fused_computation.163 | convolution fusion | flops 8685350912 | bytes 35684352 | tf_op jit(solution)/shard_map/btd,fd->btf/dot_general | solution.py:200
  504.0 16.6 %multiply_reduce_fusion.4 = (bf16[2,1024]{1,0:T(2,128)(2,1)}, f32[2,512]{1,0:T(2,128)S(1)}, bf16[2,1024]{1,0:T(2,128)(2,1)}, f32[2,512,1024]{2,1,0:T(8,128)S(1)}) fusion(f32[2,512,1024]{2,1,0:T(8,128)} %copy-done.13, f32[2,512]{1,0:T(2,128)S(1)} %fusion.83, f32[2,512]{1,0:T(2,128)S(1)} %broadcast_multiply_fusion, f32[2,1024]{1,0:T(2,128)S(1)} %copy-done.33, ...), kind=kOutput, calls=%fused_computation.101 | convolution fusion | flops 8598318080 | bytes 25194496 | tf_op jit(solution)/shard_map/btf,df->btd/dot_general | solution.py:207
  531.1 15.6 %bitcast_convert_fusion.1 = bf16[1024,4096]{1,0:T(8,128)(2,1)} fusion(bf16[2,512,4096]{2,1,0:T(8,128)(2,1)} %get-tuple-element.193, f32[2,512,1024]{2,1,0:T(8,128)} %copy-done.13, f32[2,1024]{1,0:T(2,128)S(1)} %copy-done.45, f32[2,1024]{1,0:T(2,128)S(1)} %copy-done.33, f32[2,512]{1,0:T(2,128)S(1)} %fusion.83, f32[2,512]{1,0:T(2,128)S(1)} %broadcast_multiply_fusion), kind=kOutput, calls=%fused_computation.60 | convolution fusion | flops 8599371776 | bytes 20996096 | tf_op jit(solution)/shard_map/btd,btf->df/dot_general | solution.py:203
  563.6 19.6 %bitcast_convert_fusion = bf16[4096,1024]{1,0:T(8,128)(2,1)} fusion(bf16[2,512,1024]{2,1,0:T(8,128)(2,1)} %param.19, f32[2,1024]{1,0:T(2,128)S(1)} %copy-done.28, f32[2,512,4096]{2,1,0:T(8,128)} %fusion.40, f32[4096]{0:T(1024)S(1)} %bitcast.294), kind=kOutput, calls=%fused_computation.59 | convolution fusion | flops 8639217664 | bytes 27287552 | tf_op jit(solution)/shard_map/btf,btd->fd/dot_general | solution.py:196
  597.1 199.5 %while.23 = (s32[]{:T(128)}, bf16[2,1024,3,512]{1,3,2,0:T(8,128)(2,1)}, bf16[2,1024,3,512]{1,3,2,0:T(8,128)(2,1)}, f32[2,8,1024]{2,1,0:T(8,128)}, bf16[2,1024,51...) while((s32[]{:T(128)}, bf16[2,1024,3,512]{1,3,2,0:T(8,128)(2,1)}, ...), condition=%wide.region_15.16_spmd, body=%wide.region_12.15_spmd.sunk | while | flops 5484568576 | bytes 492405792 | solution.py:223
  639.0 29.6 %multiply_convert_fusion.10 = (bf16[8,512,1024]{2,1,0:T(8,128)(2,1)}, bf16[8,512,1024]{2,1,0:T(8,128)(2,1)}) fusion(f32[8,512,1024]{2,1,0:T(8,128)} %get-tuple-element.292, f32[8,512,1024]{2,1,0:T(8,128)} %copy-done, f32[8,512]{1,0:T(8,128)} %get-tuple-element.293, f32[8,512]{1,0:T(8,128)} %get-tuple-element.287, ...), kind=kLoop, calls=%fused_computation.21.clone.1 | loop fusion | flops 41943040 | bytes 83951616 | tf_op jit(solution)/shard_map/while/body/eval_jaxpr/convert_element_type | solution.py:88
  738.4 29.3 %multiply_convert_fusion.10 = (bf16[8,512,1024]{2,1,0:T(8,128)(2,1)}, bf16[8,512,1024]{2,1,0:T(8,128)(2,1)}) fusion(f32[8,512,1024]{2,1,0:T(8,128)} %get-tuple-element.292, f32[8,512,1024]{2,1,0:T(8,128)} %copy-done, f32[8,512]{1,0:T(8,128)} %get-tuple-element.293, f32[8,512]{1,0:T(8,128)} %get-tuple-element.287, ...), kind=kLoop, calls=%fused_computation.21.clone.1 | loop fusion | flops 41943040 | bytes 83951616 | tf_op jit(solution)/shard_map/while/body/eval_jaxpr/convert_element_type | solution.py:88
  796.6 16.5 %copy.95 = bf16[2,1024,3,512]{3,0,2,1:T(2,128)(2,1)} copy(bf16[2,1024,3,512]{1,3,2,0:T(8,128)(2,1)} %get-tuple-element.65) | data formatting | bytes 12582912 | tf_op jit(solution)/shard_map/while | solution.py:223
  813.0 74.3 %all_to_all.69 = bf16[2,1024,3,512]{3,0,2,1:T(2,128)(2,1)S(1)} all-to-all(bf16[2,1024,3,512]{3,0,2,1:T(2,128)(2,1)} %copy.95), channel_id=1, replica_groups=mesh['shard'=16,'seq'=2] {'seq'}, dimensions={1} | all-to-all | bytes 12582912 | tf_op jit(solution)/shard_map/all_to_all | solution.py:226
  887.4 20.4 %copy.112 = bf16[2,2,512,3,512]{4,1,3,2,0:T(2,128)(2,1)} copy(bf16[2,2,512,3,512]{4,0,3,2,1:T(2,128)(2,1)S(1)} %bitcast.276) | data formatting | bytes 12582912 | tf_op jit(solution)/shard_map/all_to_all | solution.py:226
  907.8 15.0 %reshape.168 = bf16[2,512,3072]{2,1,0:T(8,128)(2,1)} reshape(bf16[2,512,3,2,512]{4,3,2,1,0:T(2,128)(2,1)} %bitcast.286) | data formatting | bytes 12582912 | tf_op jit(solution)/shard_map/reshape | solution.py:229
  951.0 24.3 %fusion.58 = (bf16[2,1024]{1,0:T(2,128)(2,1)S(1)}, bf16[2,1024]{1,0:T(2,128)(2,1)S(1)}, f32[2,512,1024]{2,1,0:T(8,128)}, bf16[2,512,1024]{2,1,0:T(8,128)(2,1)}) fusion(bf16[2,512,1024]{2,1,0:T(8,128)(2,1)} %param.19, f32[1024]{0:T(1024)S(1)} %convert_element_type.226, f32[2,512,1024]{2,1,0:T(8,128)} %get-tuple-element.188, f32[1024]{0:T(1024)S(1)} %copy-done.47, ...), kind=kOutput, calls=%fused_computation.99 | convolution fusion | flops 8653893632 | bytes 52498432 | tf_op jit(solution)/shard_map/btf,fd->btd/dot_general | solution.py:176
  975.4 43.1 %reduce-scatter.8.cloned.1.call-done = bf16[64,3072]{1,0:T(8,128)(2,1)} async-done(((bf16[1024,3072]{1,0:T(8,128)(2,1)}), bf16[64,3072]{1,0:T(8,128)(2,1)}) %reduce-scatter.8.cloned.1.call-update) | async-done | bytes 393232 | tf_op jit(solution)/shard_map/reduce_scatter | solution.py:269
  1050.7 57.7 %all-reduce.7 = (bf16[6144]{0:T(1024)(128)(2,1)S(1)}, bf16[2048]{0:T(1024)(128)(2,1)S(1)}, bf16[1024]{0:T(1024)(128)(2,1)S(1)}, bf16[4096]{0:T(1024)(128)(2,1)S(1)}, bf16[1024]{0:T(1024)(128)(2,1)S(1)}) all-reduce(bf16[6144]{0:T(1024)(128)(2,1)S(1)} %reduce_sum.281, ...), channel_id=3, replica_groups=mesh['shard'=16,'seq'=2] {'shard'}, use_global_device_ids=true, to_apply=%region_27.28.clone | all-reduce | flops 14336 | bytes 57344
  1132.7 78.9 %reduce-scatter.6.cloned.1.call-done = bf16[64,6144]{1,0:T(8,128)(2,1)} async-done(((bf16[1024,6144]{1,0:T(8,128)(2,1)}), bf16[64,6144]{1,0:T(8,128)(2,1)}) %reduce-scatter.6.cloned.1.call-update) | async-done | bytes 786448 | tf_op jit(solution)/shard_map/reduce_scatter | solution.py:263
  (323 shorter events, 448.5 us)
Async XLA Ops:
  7.2 106.7 %all-gather.9.cloned.1.call-start = ((), (), s32[]{:S(2)}) async-start(), calls=%async_computation.9 | async-start | bytes 13369344 | tf_op jit(solution)/shard_map/all_gather | solution.py:129
  7.9 168.3 %all-gather.11.cloned.1.call-start = ((), (), s32[]{:S(2)}) async-start(), calls=%async_computation.10 | async-start | bytes 6684672 | tf_op jit(solution)/shard_map/all_gather | solution.py:131
  8.7 445.1 %all-gather.13.cloned.1.call-start = ((), (), s32[]{:S(2)}) async-start(), calls=%async_computation.11 | async-start | bytes 2228224 | tf_op jit(solution)/shard_map/all_gather | solution.py:133
  9.4 453.8 %all-gather.15.cloned.1.call-start = ((), (), s32[]{:S(2)}) async-start(), calls=%async_computation.12 | async-start | bytes 8912896 | tf_op jit(solution)/shard_map/all_gather | solution.py:135
  54.2 122.0 %copy-start.24 = (f32[2,512]{1,0:T(2,128)}, f32[2,512]{1,0:T(2,128)S(1)}, u32[]{:S(2)}) copy-start(f32[2,512]{1,0:T(2,128)S(1)} %broadcast_multiply_fusion.1) | copy-start | bytes 12292
  56.7 119.6 %copy-start.36 = (f32[2,512]{1,0:T(2,128)}, f32[2,512]{1,0:T(2,128)S(1)}, u32[]{:S(2)}) copy-start(f32[2,512]{1,0:T(2,128)S(1)} %fusion.82) | copy-start | bytes 12292
  121.0 68.1 %copy-start.30 = (f32[2,1024]{1,0:T(2,128)}, f32[2,1024]{1,0:T(2,128)S(1)}, u32[]{:S(2)}) copy-start(f32[2,1024]{1,0:T(2,128)S(1)} %get-tuple-element.180) | copy-start | bytes 24580
  121.0 68.1 %copy-start.42 = (f32[2,1024]{1,0:T(2,128)}, f32[2,1024]{1,0:T(2,128)S(1)}, u32[]{:S(2)}) copy-start(f32[2,1024]{1,0:T(2,128)S(1)} %get-tuple-element.179) | copy-start | bytes 24580
  209.8 76.9 %all-to-all-start = ((bf16[2,512,3,1024]{1,0,2,3:T(2,128)(2,1)}), bf16[2,512,3,1024]{1,0,2,3:T(2,128)(2,1)}, u32[]{:S(2)}, u32[]{:S(2)}) async-start(bf16[2,512,3,1024]{1,0,2,3:T(2,128)(2,1)} %copy.86), calls=%async_computation | async-start | bytes 12582912 | tf_op jit(solution)/shard_map/all_to_all | solution.py:160
  216.1 263.2 %all-gather.17.cloned.1.call-start = ((), (), s32[]{:S(2)}) async-start(), calls=%async_computation.13 | async-start | bytes 8912896 | tf_op jit(solution)/shard_map/all_gather | solution.py:137
  389.1 64.6 %copy-start.10 = (bf16[2,512,1024]{2,1,0:T(8,128)(2,1)S(1)}, bf16[2,512,1024]{2,1,0:T(8,128)(2,1)}, u32[]{:S(2)}) copy-start(bf16[2,512,1024]{2,1,0:T(8,128)(2,1)} %param.17) | copy-start | bytes 6291460
  389.1 64.6 %copy-start.32 = (f32[2,1024]{1,0:T(2,128)S(1)}, f32[2,1024]{1,0:T(2,128)}, u32[]{:S(2)}) copy-start(f32[2,1024]{1,0:T(2,128)} %get-tuple-element.181) | copy-start | bytes 24580
  389.1 55.1 %all-to-all-start.1 = ((bf16[2,1024,512]{2,0,1:T(2,128)(2,1)}), bf16[2,1024,512]{2,0,1:T(2,128)(2,1)}, u32[]{:S(2)}, u32[]{:S(2)}) async-start(bf16[2,1024,512]{2,0,1:T(2,128)(2,1)} %copy.90), calls=%async_computation.1 | async-start | bytes 4194304 | tf_op jit(solution)/shard_map/all_to_all | solution.py:164
  394.1 581.3 %reduce-scatter.10.cloned.1.call-start = ((), (), s32[]{:S(2)}) async-start(), calls=%async_computation.16 | async-start | bytes 2228224 | tf_op jit(solution)/shard_map/reduce_scatter | solution.py:275
  444.2 119.4 %copy-start.38 = (f32[16,1,256]{2,1,0:T(1,128)}, f32[16,1,256]{2,1,0:T(1,128)S(1)}, u32[]{:S(2)}) copy-start(f32[16,1,256]{2,1,0:T(1,128)S(1)} %convert_element_type.251) | copy-start | bytes 49156
  531.0 444.4 %reduce-scatter.12.cloned.1.call-start = ((), (), s32[]{:S(2)}) async-start(), calls=%async_computation.17 | async-start | bytes 8912896 | tf_op jit(solution)/shard_map/reduce_scatter | solution.py:281
  559.8 29.4 %all-to-all-start.2 = ((bf16[2,512,1024]{1,0,2:T(2,128)(2,1)}), bf16[2,512,1024]{1,0,2:T(2,128)(2,1)S(1)}, u32[]{:S(2)}, u32[]{:S(2)}) async-start(bf16[2,512,1024]{1,0,2:T(2,128)(2,1)} %copy.92), calls=%async_computation.2 | async-start | bytes 4194304 | tf_op jit(solution)/shard_map/all_to_all | solution.py:222
  563.6 411.8 %reduce-scatter.14.cloned.1.call-start = ((), (), s32[]{:S(2)}) async-start(), calls=%async_computation.18 | async-start | bytes 8912896 | tf_op jit(solution)/shard_map/reduce_scatter | solution.py:287
  583.3 435.2 %reduce-scatter.8.cloned.1.call-start = ((), (), s32[]{:S(2)}) async-start(), calls=%async_computation.15 | async-start | bytes 6684672 | tf_op jit(solution)/shard_map/reduce_scatter | solution.py:269
  934.7 190.3 %all-reduce.13.cloned.1.call-start = ((), (), s32[]{:S(2)}) async-start(), calls=%async_computation.19 | async-start | bytes 3145728 | tf_op jit(solution)/shard_map/psum | solution.py:295
  951.0 67.6 %copy-start.49 = (bf16[2,1024]{1,0:T(2,128)(2,1)S(1)}, bf16[2,1024]{1,0:T(2,128)(2,1)}, u32[]{:S(2)}) copy-start(bf16[2,1024]{1,0:T(2,128)(2,1)} %get-tuple-element.106) | copy-start | bytes 12292
  951.0 67.6 %copy-start.48 = (bf16[2,1024]{1,0:T(2,128)(2,1)S(1)}, bf16[2,1024]{1,0:T(2,128)(2,1)}, u32[]{:S(2)}) copy-start(bf16[2,1024]{1,0:T(2,128)(2,1)} %get-tuple-element.102) | copy-start | bytes 12292
  951.0 76.0 %copy-start.23 = (bf16[2,1024]{1,0:T(2,128)(2,1)S(1)}, bf16[2,1024]{1,0:T(2,128)(2,1)}, u32[]{:S(2)}) copy-start(bf16[2,1024]{1,0:T(2,128)(2,1)} %param.18) | copy-start | bytes 12292
  1018.5 193.1 %reduce-scatter.6.cloned.1.call-start = ((), (), s32[]{:S(2)}) async-start(), calls=%async_computation.14 | async-start | bytes 13369344 | tf_op jit(solution)/shard_map/reduce_scatter | solution.py:263
  (63 other events, 713.0 us)
Sparse Core Ops, SparseCore 0:
  10.3 103.5 all-gather.8
  116.2 60.0 all-gather.10
  178.4 39.9 all-gather.12
  220.4 73.6 all-gather.14
  296.1 73.1 all-gather.16
  531.1 60.4 reduce-scatter.9
  596.2 103.5 reduce-scatter.11
  704.5 104.3 reduce-scatter.13
  934.8 83.6 reduce-scatter.7
  1020.8 51.3 all-reduce.12
  1076.8 134.7 reduce-scatter.5
where the time goes:
time: 1230 us; the launch traced here: 1220 us
  matrix products  356 us (29%)
  waiting for transfers between devices  313 us (25%)
  blocking collectives  235 us (19%)
  local copies, waits for them, and re-layouts  149 us (12%)
  other arithmetic  133 us (11%)
  between operations  18.1 us (1%)
  starting transfers between devices  15.4 us (1%)
    unnamed x2, blocking collectives  88.6 us
    reduce_scatter x1, waiting for transfers between devices, shards(): lax.psum_scatter(grad_ada_weight.astype(jnp.bfloat16), 'shard', scatter_d...  78.9 us
    all_to_all x1, blocking collectives, shards(): lax.all_to_all(as_sent(grad_stacked), 'seq', split_axis=1, concat_axis=3,...  74.3 us
    all_to_all x1, waiting for transfers between devices, shards(): lax.all_to_all(stacked, 'seq', split_axis=3, concat_axis=1, tiled=True)  69.9 us
    convert_element_type x2, other arithmetic, attend_back(): grad_scores = (attn_probs * (grad_probs - row_delta)).astype(jnp.bfloat16)  58.9 us
    all_gather x1, waiting for transfers between devices, shards(): lax.all_gather(ada_weight, 'shard', axis=0, tiled=True)  56.6 us
    all_gather x1, waiting for transfers between devices, shards(): lax.all_gather(qkv_weight, 'shard', axis=0, tiled=True)  55.2 us
    dot_general x4, matrix products, attend_back(): jnp.einsum('qhd,khd->hqk', grad_block, value_rows, preferred_element_type...  49 us
  transfers between devices with their start and end apart: 14, of which 6 were waited for; matrix products, arithmetic and copies ran while one was open for 46% of the time, Pallas kernels for 0%

commit v1 on v0

v1 whole, which is shorter than its diff:
```python
import functools
import math

import jax
import jax.numpy as jnp
from jax import lax
from jax.experimental import pallas as pl
from jax.experimental.pallas import tpu as pltpu
from jax.sharding import PartitionSpec as P

HD = 64
PAIR = 2 * HD
LOG2E = 1.4426950408889634
epsilon = 1e-06
f32 = jnp.float32
bf16 = jnp.bfloat16

NT = (((1,), (1,)), ((), ()))
NN = (((1,), (0,)), ((), ()))


def dot(a, b, dims=NN):
    return lax.dot_general(a, b, dims, preferred_element_type=f32)


def head_parts(block):
    lane = lax.broadcasted_iota(jnp.int32, block.shape, 1)
    zero = jnp.zeros_like(block)
    return [jnp.where(lane < HD, block, zero), jnp.where(lane < HD, zero, block)]


def attend_kernel(chunk, q_ref, k_ref, v_ref, o_ref, lse_ref):
    keys = k_ref[0]
    values_t = v_ref[0].T
    factor = LOG2E / math.sqrt(HD)

    def step(i, carry):
        rows = pl.ds(pl.multiple_of(i * chunk, chunk), chunk)
        parts = []
        for h, queries in enumerate(head_parts(q_ref[0, rows, :])):
            scores = dot(keys, queries, NT) * factor
            top = jnp.max(scores, axis=0, keepdims=True)
            shifted = jnp.exp2(scores - top)
            total = jnp.sum(shifted, axis=0, keepdims=True)
            out = dot(values_t[h * HD : (h + 1) * HD], shifted.astype(bf16))
            parts.append(out * (1.0 / total))
            lse_ref[0, 0, h : h + 1, rows] = top + jnp.log2(total)
        o_ref[0, rows, :] = jnp.concatenate(parts, 0).T.astype(bf16)
        return carry

    lax.fori_loop(0, q_ref.shape[1] // chunk, step, 0)


def attend(qkv, width):
    latents, length, _ = qkv.shape
    pairs = width // PAIR
    chunk = min(256, length)
    block = lambda at: pl.BlockSpec((1, length, PAIR), lambda l, p: (l, 0, at * pairs + p))
    elements = latents * length * length * (width // HD)
    return pl.pallas_call(
        functools.partial(attend_kernel, chunk),
        grid=(latents, pairs),
        in_specs=[block(0), block(1), block(2)],
        out_specs=[
            pl.BlockSpec((1, length, PAIR), lambda l, p: (l, 0, p)),
            pl.BlockSpec((1, 1, 2, length), lambda l, p: (l, p, 0, 0)),
        ],
        out_shape=[
            jax.ShapeDtypeStruct((latents, length, width), bf16),
            jax.ShapeDtypeStruct((latents, pairs, 2, length), f32),
        ],
        compiler_params=pltpu.CompilerParams(vmem_limit_bytes=40 * 2**20),
        cost_estimate=pl.CostEstimate(
            flops=elements * HD * 8, bytes_accessed=qkv.size * 3, transcendentals=elements
        ),
        name="attend",
    )(qkv, qkv, qkv)


def attend_back_kernel(chunk, q_ref, k_ref, v_ref, do_ref, lse_ref, g_ref, dq_s, dk_s, dv_s):
    which = pl.program_id(2)
    inverse = 1.0 / math.sqrt(HD)

    @pl.when(which == 0)
    def _():
        keys = k_ref[0]
        values = v_ref[0]
        keys_t = keys.T
        dk_s[...] = jnp.zeros_like(dk_s)
        dv_s[...] = jnp.zeros_like(dv_s)

        def step(i, carry):
            rows = pl.ds(pl.multiple_of(i * chunk, chunk), chunk)
            queries = head_parts(q_ref[0, rows, :])
            grads = head_parts(do_ref[0, rows, :])
            parts = []
            for h in range(2):
                scores = dot(keys, queries[h], NT) * (LOG2E * inverse)
                probs = jnp.exp2(scores - lse_ref[0, 0, h : h + 1, rows])
                g_probs = dot(values, grads[h], NT)
                delta = jnp.sum(probs * g_probs, axis=0, keepdims=True)
                g_scores = (probs * (g_probs - delta)).astype(bf16)
                dv_s[...] += dot(probs.astype(bf16), grads[h])
                dk_s[...] += dot(g_scores, queries[h])
                parts.append(dot(keys_t[h * HD : (h + 1) * HD], g_scores))
            dq_s[rows, :] = (jnp.concatenate(parts, 0).T * inverse).astype(bf16)
            return carry

        lax.fori_loop(0, q_ref.shape[1] // chunk, step, 0)
        g_ref[0] = dq_s[...]

    @pl.when(which == 1)
    def _():
        g_ref[0] = (dk_s[...] * inverse).astype(bf16)

    @pl.when(which == 2)
    def _():
        g_ref[0] = dv_s[...].astype(bf16)


def attend_back(qkv, g_attended, lse):
    latents, length, width = g_attended.shape
    pairs = width // PAIR
    chunk = min(256, length)
    block = lambda at: pl.BlockSpec((1, length, PAIR), lambda l, p, w: (l, 0, at * pairs + p))
    elements = latents * length * length * (width // HD)
    return pl.pallas_call(
        functools.partial(attend_back_kernel, chunk),
        grid=(latents, pairs, 3),
        in_specs=[
            block(0),
            block(1),
            block(2),
            block(0),
            pl.BlockSpec((1, 1, 2, length), lambda l, p, w: (l, p, 0, 0)),
        ],
        out_specs=pl.BlockSpec((1, length, PAIR), lambda l, p, w: (l, 0, w * pairs + p)),
        out_shape=jax.ShapeDtypeStruct((latents, length, 3 * width), bf16),
        scratch_shapes=[
            pltpu.VMEM((length, PAIR), bf16),
            pltpu.VMEM((length, PAIR), f32),
            pltpu.VMEM((length, PAIR), f32),
        ],
        compiler_params=pltpu.CompilerParams(vmem_limit_bytes=40 * 2**20),
        cost_estimate=pl.CostEstimate(
            flops=elements * HD * 20, bytes_accessed=qkv.size * 4, transcendentals=elements
        ),
        name="attend_back",
    )(qkv, qkv, qkv, g_attended, lse)


def modulate(residual, shift, scale):
    average = jnp.mean(residual, -1, keepdims=True)
    centred = residual - average
    spread = jnp.mean(centred * centred, -1, keepdims=True)
    return centred * lax.rsqrt(spread + epsilon) * (1.0 + scale[:, None, :]) + shift[:, None, :]


def gelu_tanh(values):
    return jax.nn.gelu(values, approximate=True)


def swap_in(x, parts):
    if parts == 1:
        return x
    if parts != 2:
        return lax.all_to_all(x, "seq", split_axis=0, concat_axis=1, tiled=True)
    here = lax.axis_index("seq")
    own = x.shape[0] // 2
    mine = lax.dynamic_slice_in_dim(x, here * own, own, 0)
    other = lax.dynamic_slice_in_dim(x, (1 - here) * own, own, 0)
    return jnp.concatenate([mine, lax.ppermute(other, "seq", [(0, 1), (1, 0)])], 1)


def swap_out(x, parts):
    if parts == 1:
        return x
    if parts != 2:
        sent = lax.all_to_all(x.astype(bf16), "seq", split_axis=1, concat_axis=0, tiled=True)
        return sent.astype(x.dtype)
    here = lax.axis_index("seq")
    rows = x.shape[1] // 2
    mine = x[:, :rows]
    other = lax.ppermute(x[:, rows:].astype(bf16), "seq", [(0, 1), (1, 0)]).astype(x.dtype)
    return jnp.where(
        here == 0, jnp.concatenate([mine, other], 0), jnp.concatenate([other, mine], 0)
    )


def gather_rows(x):
    return lax.all_gather(x, "shard", axis=0, tiled=True)


def seq_sum(x, parts):
    if parts == 2:
        return x.astype(f32) + lax.ppermute(x, "seq", [(0, 1), (1, 0)]).astype(f32)
    return lax.psum(x.astype(f32), "seq")


def scatter_rows(g, parts):
    own = lax.psum_scatter(g.astype(bf16), "shard", scatter_dimension=0, tiled=True)
    return seq_sum(own, parts)


def shards(
    shape,
    tokens,
    condition,
    cotangent,
    ada_weight,
    ada_bias,
    qkv_weight,
    qv_bias,
    proj_weight,
    proj_bias,
    up_weight,
    up_bias,
    down_weight,
    down_bias,
):
    n, parts = shape["shard"], shape["seq"]
    shard, seq = lax.axis_index("shard"), lax.axis_index("seq")
    latents, local_rows, width = tokens.shape
    own = latents // parts
    columns = ada_weight.shape[0]
    ff = down_weight.shape[0] * n

    biases = (qv_bias, proj_bias, up_bias, down_bias)
    sizes = [b.shape[0] for b in biases]
    w_qkv = gather_rows(qkv_weight)
    tokens_own = swap_in(tokens, parts)
    all_biases = lax.all_gather(jnp.concatenate(biases), "shard", axis=0, tiled=False).astype(f32)
    offsets = [sum(sizes[:i]) for i in range(5)]
    b_qv, b_proj, b_up, b_down = [
        all_biases[:, offsets[i] : offsets[i + 1]].reshape(-1) for i in range(4)
    ]

    cond_float = condition.astype(f32)
    cond_act = jax.nn.silu(cond_float).astype(bf16)
    cond_cols = lax.all_to_all(
        cond_act.reshape(latents, n, columns).transpose(1, 0, 2), "shard", 0, 0, tiled=True
    )
    cond_cols = cond_cols.reshape(n, latents, columns)
    cond_block = lax.dynamic_slice_in_dim(cond_cols, seq * own, own, 1).reshape(n * own, columns)
    partial = dot(cond_block, ada_weight)
    span = ada_bias.shape[0]
    owned = lax.broadcasted_iota(jnp.int32, (1, n, 1), 1) == shard
    bias_row = jnp.where(owned, ada_bias.astype(f32)[None, None, :], 0.0).reshape(1, n * span)
    partial = (partial + bias_row).reshape(n, own * n * span)
    arrived = lax.all_to_all(partial, "shard", 0, 0, tiled=True)
    modulation = jnp.sum(arrived, axis=0).reshape(own, n * span)
    shift_one, scale_one, gate_one, shift_two, scale_two, gate_two = jnp.split(
        modulation, 6, axis=1
    )

    w_proj = gather_rows(proj_weight)
    w_up = gather_rows(up_weight)
    w_down = gather_rows(down_weight)
    cot_own = swap_in(cotangent, parts)

    residual = tokens_own.astype(f32)
    normed_one = modulate(residual, shift_one, scale_one).astype(bf16)
    zero = jnp.zeros((width,), f32)
    qkv_bias = jnp.concatenate([b_qv[:width], zero, b_qv[width:]])
    qkv = (
        jnp.einsum("btd,de->bte", normed_one, w_qkv, preferred_element_type=f32) + qkv_bias
    ).astype(bf16)
    attended, lse = attend(qkv, width)
    branch = jnp.einsum("bte,ed->btd", attended, w_proj, preferred_element_type=f32) + b_proj
    middle = residual + gate_one[:, None, :] * branch
    normed_two = modulate(middle, shift_two, scale_two).astype(bf16)
    hidden = jnp.einsum("btd,df->btf", normed_two, w_up, preferred_element_type=f32) + b_up
    active = gelu_tanh(hidden).astype(bf16)
    output = jnp.einsum("btf,fd->btd", active, w_down, preferred_element_type=f32) + b_down
    result = swap_out((middle + gate_two[:, None, :] * output).astype(bf16), parts)

    grad_result = cot_own.astype(f32)
    grad_output = (gate_two[:, None, :] * grad_result).astype(bf16)
    grad_gate_two = jnp.sum(grad_result * output, axis=1)
    grad_down_weight = scatter_rows(
        jnp.einsum("btf,btd->fd", active, grad_output, preferred_element_type=f32), parts
    )
    grad_down_bias = jnp.sum(grad_output, axis=(0, 1), dtype=f32)
    grad_active = jnp.einsum("btd,fd->btf", grad_output, w_down, preferred_element_type=f32)
    unused, gelu_back = jax.vjp(gelu_tanh, hidden)
    grad_hidden = gelu_back(grad_active)[0].astype(bf16)
    grad_up_weight = scatter_rows(
        jnp.einsum("btd,btf->df", normed_two, grad_hidden, preferred_element_type=f32), parts
    )
    grad_up_bias = jnp.sum(grad_hidden, axis=(0, 1), dtype=f32)
    grad_normed_two = jnp.einsum("btf,df->btd", grad_hidden, w_up, preferred_element_type=f32)
    unused, norm_back_two = jax.vjp(modulate, middle, shift_two, scale_two)
    grad_middle, grad_shift_two, grad_scale_two = norm_back_two(grad_normed_two)
    grad_middle = grad_middle + grad_result
    grad_branch = (gate_one[:, None, :] * grad_middle).astype(bf16)
    grad_gate_one = jnp.sum(grad_middle * branch, axis=1)
    grad_proj_weight = scatter_rows(
        jnp.einsum("bte,btd->ed", attended, grad_branch, preferred_element_type=f32), parts
    )
    grad_proj_bias = jnp.sum(grad_branch, axis=(0, 1), dtype=f32)
    grad_attended = jnp.einsum(
        "btd,ed->bte", grad_branch, w_proj, preferred_element_type=f32
    ).astype(bf16)
    grad_qkv = attend_back(qkv, grad_attended, lse)
    grad_qkv_weight = scatter_rows(
        jnp.einsum("btd,bte->de", normed_one, grad_qkv, preferred_element_type=f32), parts
    )
    column_sums = jnp.sum(grad_qkv, axis=(0, 1), dtype=f32)
    grad_qv_bias = jnp.concatenate([column_sums[:width], column_sums[2 * width :]])
    grad_normed_one = jnp.einsum("bte,de->btd", grad_qkv, w_qkv, preferred_element_type=f32)
    unused, norm_back_one = jax.vjp(modulate, residual, shift_one, scale_one)
    grad_input, grad_shift_one, grad_scale_one = norm_back_one(grad_normed_one)
    grad_tokens = swap_out(grad_input + grad_middle, parts)

    grad_modulation = jnp.concatenate(
        [
            grad_shift_one,
            grad_scale_one,
            grad_gate_one,
            grad_shift_two,
            grad_scale_two,
            grad_gate_two,
        ],
        axis=1,
    ).astype(bf16)
    bias_grads = jnp.concatenate(
        [
            g.reshape(n, -1)
            for g in (grad_qv_bias, grad_proj_bias, grad_up_bias, grad_down_bias)
        ],
        axis=1,
    ).astype(bf16)
    total = sum(sizes)
    sent = jnp.concatenate([grad_modulation.reshape(-1), bias_grads.reshape(-1)])
    everyone = lax.all_gather(sent, ("shard", "seq"), axis=0, tiled=False)
    everyone = everyone.reshape(n * parts, -1)
    all_modulation = everyone[:, : own * n * span].reshape(n * latents, n * span)
    own_biases = jnp.sum(
        lax.dynamic_slice_in_dim(everyone, own * n * span + shard * total, total, 1).astype(f32),
        axis=0,
    )
    grad_qv, grad_proj, grad_up, grad_down = [
        own_biases[offsets[i] : offsets[i + 1]] for i in range(4)
    ]
    grad_ada_weight = lax.dot_general(
        cond_cols.reshape(n * latents, columns),
        all_modulation,
        (((0,), (0,)), ((), ())),
        preferred_element_type=f32,
    )
    grad_ada_bias = jnp.sum(
        lax.dynamic_slice_in_dim(all_modulation, shard * span, span, 1).astype(f32), axis=0
    )
    grad_cond_cols = dot(all_modulation, ada_weight, NT).reshape(n, latents * columns)
    grad_cond_act = lax.all_to_all(grad_cond_cols, "shard", 0, 0, tiled=True)
    grad_cond_act = (
        grad_cond_act.reshape(n, latents, columns).transpose(1, 0, 2).reshape(latents, width)
    )
    unused, silu_back = jax.vjp(jax.nn.silu, cond_float)
    grad_condition = silu_back(grad_cond_act)[0]
    return (
        result,
        grad_tokens,
        grad_condition,
        grad_ada_weight,
        grad_ada_bias,
        grad_qkv_weight,
        grad_qv,
        grad_proj_weight,
        grad_proj,
        grad_up_weight,
        grad_up,
        grad_down_weight,
        grad_down,
    )


def solution(mesh):
    rows, flat = P("shard", None), P("shard")
    split = P("shard", "seq", None)
    in_specs = (split, rows, split) + (rows, flat) * 5
    out_specs = (split, split, rows) + (rows, flat) * 5
    body = functools.partial(shards, dict(mesh.shape))
    return jax.shard_map(
        body, mesh=mesh, in_specs=in_specs, out_specs=out_specs, check_vma=False
    )
```

time: 1230 us -> 775 us (0.63)
  matrix products: 356 us -> 159 us
  Pallas kernels: 0 us -> 129 us
  blocking collectives: 235 us -> 116 us
  local copies, waits for them, and re-layouts: 149 us -> 52.2 us
  other arithmetic: 133 us -> 47.7 us
  waiting for transfers between devices: 313 us -> 228 us
    dot_general x42 -> x14, matrix products: 340 us -> 144 us  [the longest x1 27.5 us: shards(): jnp.einsum('btd,fd->btf', grad_output, w_down, preferred_element_type=f32)]
    pallas_call x0 -> x2, Pallas kernels: none -> 129 us  [the longest x1 75.4 us: attend_back(): pl.pallas_call(functools.partial(attend_back_kernel, chunk), grid=(latent...]
    unnamed x2 -> x0, blocking collectives: 88.6 us -> none
    convert_element_type x18 -> x2, other arithmetic: 79.9 us -> 1.53 us  [the longest x1 1.51 us: swap_out(): lax.ppermute(x[:, rows:].astype(bf16), 'seq', [(0, 1), (1, 0)])]
    all_to_all x1 -> x0, blocking collectives: 74.3 us -> none  [shards(): lax.all_to_all(as_sent(grad_stacked), 'seq', split_axis=1, concat_axis=3,...]
    all_to_all x3, waiting for transfers between devices: 75.8 us -> 14.9 us  [the longest x1 14.3 us: shards(): arrived = lax.all_to_all(partial, 'shard', 0, 0, tiled=True)]
    all_gather x3 -> x2, blocking collectives: 58.8 us -> 116 us  [the longest x1 94.2 us: shards(): everyone = lax.all_gather(sent, ('shard', 'seq'), axis=0, tiled=False)]
    all_to_all x7 -> x3, local copies, waits for them, and re-layouts: 53.4 us -> 2.36 us  [the longest x2 1.2 us: shards(): grad_cond_act = lax.all_to_all(grad_cond_cols, 'shard', 0, 0, tiled=True)]
  transfers between devices with their start and end apart: 14 -> 19, of which waited for: 6 -> 8; matrix products, arithmetic and copies ran while one was open for 46% -> 21% of each run, Pallas kernels for 0% -> 17%
where the time goes in v1:
time: 775 us; the launch traced here: 771 us
  waiting for transfers between devices  228 us (29%)
  matrix products  159 us (21%)
  Pallas kernels  129 us (17%)
  blocking collectives  116 us (15%)
  local copies, waits for them, and re-layouts  52.2 us (7%)
  other arithmetic  47.7 us (6%)
  starting transfers between devices  24.3 us (3%)
  between operations  15.1 us (2%)
    all_gather x4, waiting for transfers between devices, gather_rows(): return lax.all_gather(x, 'shard', axis=0, tiled=True)  101 us
    all_gather x1, blocking collectives, shards(): everyone = lax.all_gather(sent, ('shard', 'seq'), axis=0, tiled=False)  94.2 us
    reduce_scatter x4, waiting for transfers between devices, scatter_rows(): lax.psum_scatter(g.astype(bf16), 'shard', scatter_dimension=0, tiled=True)  93.3 us
    pallas_call x1, Pallas kernels, attend_back(): pl.pallas_call(functools.partial(attend_back_kernel, chunk), grid=(latent...  75.4 us
    pallas_call x1, Pallas kernels, attend(): pl.pallas_call(functools.partial(attend_kernel, chunk), grid=(latents, pa...  53.5 us
    dot_general x1, matrix products, shards(): jnp.einsum('btd,fd->btf', grad_output, w_down, preferred_element_type=f32)  27.5 us
    unnamed x107, local copies, waits for them, and re-layouts  26.6 us
    all_gather x1, blocking collectives, shards(): lax.all_gather(jnp.concatenate(biases), 'shard', axis=0, tiled=False)  22.2 us
  transfers between devices with their start and end apart: 19, of which 8 were waited for; matrix products, arithmetic and copies ran while one was open for 21% of the time, Pallas kernels for 17%

profile of v1, /device:TPU:0, one launch (start us, length us, event | category | flops | bytes accessed | tf_op | source)
XLA Modules:
  0.0 771.3 jit_solution(6258641703128732830)
XLA Ops:
  19.2 5.9 all-to-all-start
  28.8 22.2 %all-gather.2 = bf16[16,1,512]{2,1,0:T(2,128)(2,1)S(1)} all-gather(bf16[1,1,512]{2,1,0:T(2,128)(2,1)S(1)} %reshape.674), channel_id=2, replica_groups=mesh['shard'=16,'seq'=2] {'shard'}, dimensions={0}, use_global_device_ids=true | all-gather | bytes 17408 | tf_op jit(solution)/shard_map/all_gather | solution.py:232
  59.2 14.3 %all-to-all-done.1 = f32[16,1,6144]{2,1,0:T(1,128)S(1)} async-done(((f32[16,1,6144]{2,1,0:T(1,128)}), f32[16,1,6144]{2,1,0:T(1,128)S(1)}, u32[]{:S(2)}, u32[]{:S(2)}) %all-to-all-start.1) | async-done | bytes 393248 | tf_op jit(solution)/shard_map/all_to_all | solution.py:250
  75.3 5.8 all-gather.8.cloned.1.call-done
  81.2 10.5 %fusion.8.q_ref.k_ref.v_ref = bf16[1,1024,3072]{2,1,0:T(8,128)(2,1)S(1)} fusion(f32[3072]{0:T(1024)S(1)} %pad_maximum_fusion.3, bf16[1024,3072]{1,0:T(8,128)(2,1)} %all-gather.8.cloned.1.call-done, f32[1024]{0:T(1024)S(1)} %bitcast.125, f32[1024]{0:T(1024)S(1)} %bitcast.105, f32[1024]{0:T(1024)S(1)} %fusion.50, f32[1024]{0:T(1024)S(1)} %broadcast_multiply_fusion.1, ...), kind=kOutput, calls=%fused_computation.15 | convolution fusion | flops 6458179584 | bytes 14708736 | tf_op jit(solution)/shard_map/btd,de->bte/dot_general | solution.py:266
  91.7 53.5 %attend.1 = (bf16[1,1024,1024]{2,1,0:T(8,128)(2,1)S(1)}, f32[1,8,2,1024]{3,2,1,0:T(2,128)S(1)}) custom-call(bf16[1,1024,3072]{2,1,0:T(8,128)(2,1)S(1)} %fusion.8.q_ref.k_ref.v_ref, bf16[1,1024,3072]{2,1,0:T(8,128)(2,1)S(1)} %fusion.8.q_ref.k_ref.v_ref, bf16[1,1024,3072]{2,1,0:T(8,128)(2,1)S(1)} %fusion.8.q_ref.k_ref.v_ref), custom_call_target="tpu_custom_call" | custom-call | flops 8589934592 | bytes 9437184 | tf_op jit(solution)/shard_map/attend/pallas_call | solution.py:60
  147.8 7.2 fusion.61
  157.5 42.2 %all-gather.12.cloned.1.call-done = bf16[1024,4096]{1,0:T(8,128)(2,1)} async-done(((bf16[64,4096]{1,0:T(8,128)(2,1)}), bf16[1024,4096]{1,0:T(8,128)(2,1)}) %all-gather.12.cloned.1.call-update) | async-done | bytes 8388624 | tf_op jit(solution)/shard_map/all_gather | solution.py:191
  199.6 22.2 %multiply_convert_fusion = (bf16[1024,4096]{1,0:T(8,128)(2,1)}, f32[1024,4096]{1,0:T(8,128)}) fusion(f32[4096]{0:T(1024)S(1)} %bitcast.121, bf16[1024,4096]{1,0:T(8,128)(2,1)} %all-gather.12.cloned.1.call-done, f32[1024,1024]{0,1:T(8,128)} %copy-done.4, f32[1024]{0:T(1024)S(1)} %bitcast.123, f32[1024]{0:T(1024)S(1)} %bitcast.114, f32[1024]{0:T(1024)S(1)} %fusion.51, ...), kind=kOutput, calls=%fused_computation.9 | convolution fusion | flops 8637120512 | bytes 37781504 | tf_op jit(solution)/shard_map/btd,df->btf/dot_general | solution.py:272
  221.8 53.0 %all-gather.14.cloned.1.call-done = bf16[4096,1024]{1,0:T(8,128)(2,1)} async-done(((bf16[256,1024]{1,0:T(8,128)(2,1)}), bf16[4096,1024]{1,0:T(8,128)(2,1)}) %all-gather.14.cloned.1.call-update) | async-done | bytes 8388624 | tf_op jit(solution)/shard_map/all_gather | solution.py:191
  274.8 27.5 %fusion.68 = (bf16[4096]{0:T(1024)(128)(2,1)}, bf16[1024,4096]{1,0:T(8,128)(2,1)}) fusion(f32[1024,4096]{1,0:T(8,128)} %get-tuple-element.131, f32[4096]{0:T(1024)S(1)} %bitcast.122, bf16[4096,1024]{1,0:T(8,128)(2,1)} %all-gather.14.cloned.1.call-done, f32[1024]{0:T(1024)S(1)} %bitcast.110, bf16[512,1024]{0,1:T(8,128)(2,1)} %bitcast.18, ...), kind=kOutput, calls=%fused_computation.134 | convolution fusion | flops 8688496640 | bytes 35680256 | tf_op jit(solution)/shard_map/btd,fd->btf/dot_general | solution.py:284
  302.4 13.3 %fusion.67 = (bf16[1024]{0:T(1024)(128)(2,1)}, f32[1024,1024]{1,0:T(8,128)}) fusion(bf16[1024,4096]{1,0:T(8,128)(2,1)} %get-tuple-element.137, bf16[1024,4096]{1,0:T(8,128)(2,1)S(1)} %copy-done.44), kind=kOutput, calls=%fused_computation.133 | convolution fusion | flops 8590982144 | bytes 20973568 | tf_op jit(solution)/shard_map/btf,df->btd/dot_general | solution.py:291
  315.6 5.7 copy.103
  326.6 15.2 %fusion.69 = f32[1024,1024]{0,1:T(8,128)} fusion(bf16[1024,4096]{1,0:T(8,128)(2,1)} %get-tuple-element.130, bf16[4096,1024]{1,0:T(8,128)(2,1)} %all-gather.14.cloned.1.call-done), kind=kOutput, calls=%fused_computation.135 | convolution fusion | flops 8589934592 | bytes 20971520 | tf_op jit(solution)/shard_map/btf,fd->btd/dot_general | solution.py:274
  341.8 5.4 fusion.60
  359.9 75.4 %attend_back.1 = bf16[1,1024,3072]{2,1,0:T(8,128)(2,1)S(1)} custom-call(bf16[1,1024,3072]{2,1,0:T(8,128)(2,1)} %copy-done.2, bf16[1,1024,3072]{2,1,0:T(8,128)(2,1)} %copy-done.2, bf16[1,1024,3072]{2,1,0:T(8,128)(2,1)} %copy-done.2, bf16[1,1024,1024]{2,1,0:T(8,128)(2,1)S(1)} %convert_bitcast_fusion.do_ref, f32[1,8,2,1024]{3,2,1,0:T(2,128)S(1)} %get-tuple-element.16.lse_ref), custom_call_target="tpu_custom_call" | custom-call | flops 21474836480 | bytes 12582912 | tf_op jit(solution)/shard_map/attend_back/pallas_call | solution.py:127
  437.9 9.0 %fusion.13 = bf16[1024,3072]{1,0:T(8,128)(2,1)} fusion(bf16[1,1024,3072]{2,1,0:T(8,128)(2,1)S(1)} %attend_back.1, f32[1024]{0:T(1024)S(1)} %bitcast.126, f32[1024]{0:T(1024)S(1)} %bitcast.106, f32[1024]{0:T(1024)S(1)} %copy-done.29, f32[1024]{0:T(1024)S(1)} %copy-done.21, bf16[512,1024]{0,1:T(8,128)(2,1)S(1)} %bitcast.90, bf16[512,1024]{0,1:T(8,128)(2,1)S(1)} %bitcast.84), kind=kOutput, calls=%fused_computation.25 | convolution fusion | flops 6455033856 | bytes 14696448 | tf_op jit(solution)/shard_map/btd,bte->de/dot_general | solution.py:306
  447.0 15.6 %convolution_convert_fusion.1 = bf16[1024,4096]{1,0:T(8,128)(2,1)} fusion(bf16[1024,4096]{1,0:T(8,128)(2,1)} %get-tuple-element.137, f32[1024,1024]{0,1:T(8,128)} %copy-done.4, f32[1024]{0:T(1024)S(1)} %bitcast.124, f32[1024]{0:T(1024)S(1)} %bitcast.117, f32[1024]{0:T(1024)S(1)} %fusion.51, f32[1024]{0:T(1024)S(1)} %broadcast_multiply_fusion), kind=kOutput, calls=%fused_computation.12 | convolution fusion | flops 8599371776 | bytes 20987904 | tf_op jit(solution)/shard_map/btd,btf->df/dot_general | solution.py:288
  462.7 16.2 %convolution_convert_fusion = bf16[4096,1024]{1,0:T(8,128)(2,1)} fusion(bf16[1024,4096]{1,0:T(8,128)(2,1)} %get-tuple-element.130, f32[1024]{0:T(1024)S(1)} %bitcast.112, bf16[512,1024]{0,1:T(8,128)(2,1)} %bitcast.18, bf16[512,1024]{0,1:T(8,128)(2,1)} %bitcast.95), kind=kOutput, calls=%fused_computation.11 | convolution fusion | flops 8600420352 | bytes 18878464 | tf_op jit(solution)/shard_map/btf,btd->fd/dot_general | solution.py:281
  485.0 12.1 %fusion.66 = (bf16[1024]{0:T(1024)(128)(2,1)S(1)}, f32[1024,1024]{1,0:T(8,128)}) fusion(bf16[1024,3072]{1,0:T(8,128)(2,1)} %all-gather.8.cloned.1.call-done, bf16[1,1024,3072]{2,1,0:T(8,128)(2,1)} %copy-done.1), kind=kOutput, calls=%fused_computation.132 | convolution fusion | flops 6443498496 | bytes 16779264 | tf_op jit(solution)/shard_map/bte,de->btd/dot_general | solution.py:310
  508.8 5.7 fusion.28
  519.3 94.2 %all-gather.1 = bf16[458752]{0:T(1024)(128)(2,1)S(1)} all-gather(bf16[14336]{0:T(1024)(128)(2,1)S(1)} %constant_dynamic-update-slice_fusion), channel_id=3, replica_groups=mesh['shard'=16,'seq'=2] {'shard','seq'}, dimensions={0}, use_global_device_ids=true | all-gather | bytes 946176 | tf_op jit(solution)/shard_map/all_gather | solution.py:335
  654.8 93.3 %reduce-scatter.11.cloned.1.call-done = bf16[256,1024]{1,0:T(8,128)(2,1)} async-done(((bf16[4096,1024]{1,0:T(8,128)(2,1)}), bf16[256,1024]{1,0:T(8,128)(2,1)}) %reduce-scatter.11.cloned.1.call-update) | async-done | bytes 524304 | tf_op jit(solution)/shard_map/reduce_scatter | solution.py:201
  751.7 10.3 %collective-permute-done.7 = bf16[256,1024]{1,0:T(8,128)(2,1)S(1)} collective-permute-done((bf16[256,1024]{1,0:T(8,128)(2,1)}, bf16[256,1024]{1,0:T(8,128)(2,1)S(1)}, u32[]{:S(2)}, u32[]{:S(2)}) %collective-permute-start.7) | collective-permute-done | bytes 524320 | tf_op jit(solution)/shard_map/ppermute | solution.py:196
  (221 shorter events, 120.4 us)
Async XLA Ops:
  7.2 74.0 %all-gather.8.cloned.1.call-start = ((), (), s32[]{:S(2)}) async-start(), calls=%async_computation.7 | async-start | bytes 6684672 | tf_op jit(solution)/shard_map/all_gather | solution.py:191
  7.9 139.9 %all-gather.10.cloned.1.call-start = ((), (), s32[]{:S(2)}) async-start(), calls=%async_computation.8 | async-start | bytes 2228224 | tf_op jit(solution)/shard_map/all_gather | solution.py:191
  8.7 190.9 %all-gather.12.cloned.1.call-start = ((), (), s32[]{:S(2)}) async-start(), calls=%async_computation.9 | async-start | bytes 8912896 | tf_op jit(solution)/shard_map/all_gather | solution.py:191
  9.4 265.4 %all-gather.14.cloned.1.call-start = ((), (), s32[]{:S(2)}) async-start(), calls=%async_computation.10 | async-start | bytes 8912896 | tf_op jit(solution)/shard_map/all_gather | solution.py:191
  15.5 58.2 %collective-permute-start = (bf16[1,512,1024]{1,2,0:T(8,128)(2,1)}, bf16[1,512,1024]{1,2,0:T(8,128)(2,1)S(1)}, u32[]{:S(2)}, u32[]{:S(2)}) collective-permute-start(bf16[1,512,1024]{1,2,0:T(8,128)(2,1)} %copy.114), channel_id=1, source_target_pairs={{0,1},{1,0},{2,3},{3,2},{4,5},{5,4},{6,7},{7,6},{8,9},{9,8},{10,11... | collective-permute-start | bytes 3145736 | tf_op jit(solution)/shard_map/ppermute | solution.py:172
  19.2 31.8 %all-to-all-start = ((bf16[16,2,64]{2,1,0:T(2,128)(2,1)}), bf16[16,2,64]{2,1,0:T(2,128)(2,1)S(1)}, u32[]{:S(2)}, u32[]{:S(2)}) async-start(bf16[16,2,64]{2,1,0:T(2,128)(2,1)} %copy.97), calls=%async_computation | async-start | bytes 16384 | tf_op jit(solution)/shard_map/all_to_all | solution.py:240
  26.4 195.3 %collective-permute-start.2 = (bf16[1,512,1024]{1,2,0:T(8,128)(2,1)}, bf16[1,512,1024]{1,2,0:T(8,128)(2,1)}, u32[]{:S(2)}, u32[]{:S(2)}) collective-permute-start(bf16[1,512,1024]{1,2,0:T(8,128)(2,1)} %copy.117), channel_id=1, source_target_pairs={{0,1},{1,0},{2,3},{3,2},{4,5},{5,4},{6,7},{7,6},{8,9},{9,8},{10,11... | collective-permute-start | bytes 3145736 | tf_op jit(solution)/shard_map/ppermute | solution.py:172
  52.4 21.0 %all-to-all-start.1 = ((f32[16,1,6144]{2,1,0:T(1,128)}), f32[16,1,6144]{2,1,0:T(1,128)S(1)}, u32[]{:S(2)}, u32[]{:S(2)}) async-start(f32[16,1,6144]{2,1,0:T(1,128)} %copy.99), calls=%async_computation.1 | async-start | bytes 786432 | tf_op jit(solution)/shard_map/all_to_all | solution.py:250
  56.0 581.7 %reduce-scatter.7.cloned.1.call-start = ((), (), s32[]{:S(2)}) async-start(), calls=%async_computation.12 | async-start | bytes 2228224 | tf_op jit(solution)/shard_map/reduce_scatter | solution.py:201
  56.7 91.1 %copy-start.32 = (f32[1024]{0:T(1024)}, f32[1024]{0:T(1024)S(1)}, u32[]{:S(2)}) copy-start(f32[1024]{0:T(1024)S(1)} %add.210) | copy-start | bytes 12292
  355.2 284.6 %reduce-scatter.5.cloned.1.call-start = ((), (), s32[]{:S(2)}) async-start(), calls=%async_computation.11 | async-start | bytes 6684672 | tf_op jit(solution)/shard_map/reduce_scatter | solution.py:201
  359.8 78.1 %copy-start.9 = (bf16[1,512,1024]{1,2,0:T(8,128)(2,1)S(1)}, bf16[1,512,1024]{1,2,0:T(8,128)(2,1)}, u32[]{:S(2)}) copy-start(bf16[1,512,1024]{1,2,0:T(8,128)(2,1)} %copy-done.8) | copy-start | bytes 3145732
  359.8 78.1 %copy-start.11 = (bf16[1,512,1024]{1,2,0:T(8,128)(2,1)S(1)}, bf16[1,512,1024]{1,2,0:T(8,128)(2,1)}, u32[]{:S(2)}) copy-start(bf16[1,512,1024]{1,2,0:T(8,128)(2,1)} %copy-done.10) | copy-start | bytes 3145732
  446.9 198.6 %reduce-scatter.9.cloned.1.call-start = ((), (), s32[]{:S(2)}) async-start(), calls=%async_computation.13 | async-start | bytes 8912896 | tf_op jit(solution)/shard_map/reduce_scatter | solution.py:201
  462.6 285.4 %reduce-scatter.11.cloned.1.call-start = ((), (), s32[]{:S(2)}) async-start(), calls=%async_computation.14 | async-start | bytes 8912896 | tf_op jit(solution)/shard_map/reduce_scatter | solution.py:201
  514.5 98.9 %copy-start.15 = (bf16[1,1024,1024]{1,2,0:T(8,128)(2,1)S(1)}, bf16[1,1024,1024]{1,2,0:T(8,128)(2,1)}, u32[]{:S(2)}) copy-start(bf16[1,1024,1024]{1,2,0:T(8,128)(2,1)} %get-tuple-element.108) | copy-start | bytes 6291460
  517.8 102.2 %copy-start.23 = (bf16[16,2,64]{2,1,0:T(2,128)(2,1)S(1)}, bf16[16,2,64]{2,1,0:T(2,128)(2,1)}, u32[]{:S(2)}) copy-start(bf16[16,2,64]{2,1,0:T(2,128)(2,1)} %copy-done.22) | copy-start | bytes 12292
  517.8 110.5 %collective-permute-start.3 = (bf16[1,512,1024]{1,2,0:T(8,128)(2,1)}, bf16[1,512,1024]{1,2,0:T(8,128)(2,1)}, u32[]{:S(2)}, u32[]{:S(2)}) collective-permute-start(bf16[1,512,1024]{1,2,0:T(8,128)(2,1)} %slice.122), channel_id=1, source_target_pairs={{0,1},{1,0},{2,3},{3,2},{4,5},{5,4},{6,7},{7,6},{8,9},{9,8},{10,11... | collective-permute-start | bytes 3145736 | tf_op jit(solution)/shard_map/ppermute | solution.py:184
  615.4 24.4 %collective-permute-start.1 = (bf16[1,512,1024]{1,2,0:T(8,128)(2,1)}, bf16[1,512,1024]{1,2,0:T(8,128)(2,1)}, u32[]{:S(2)}, u32[]{:S(2)}) collective-permute-start(bf16[1,512,1024]{1,2,0:T(8,128)(2,1)} %get-tuple-element.112), channel_id=1, source_target_pairs={{0,1},{1,0},{2,3},{3,2},{4,5},{5,4},{6,7},{7,6},{8,9},{9,8},{10,11... | collective-permute-start | bytes 3145736 | tf_op jit(solution)/shard_map/ppermute | solution.py:184
  616.5 9.9 %all-to-all-start.2 = ((f32[16,1,128]{2,1,0:T(1,128)}), f32[16,1,128]{2,1,0:T(1,128)S(1)}, u32[]{:S(2)}, u32[]{:S(2)}) async-start(f32[16,1,128]{2,1,0:T(1,128)} %bitcast.24), calls=%async_computation.2 | async-start | bytes 16384 | tf_op jit(solution)/shard_map/all_to_all | solution.py:355
  637.7 7.1 collective-permute-start.5
  639.7 13.1 %collective-permute-start.4 = (bf16[64,3072]{1,0:T(8,128)(2,1)}, bf16[64,3072]{1,0:T(8,128)(2,1)}, u32[]{:S(2)}, u32[]{:S(2)}) collective-permute-start(bf16[64,3072]{1,0:T(8,128)(2,1)} %reduce-scatter.5.cloned.1.call-done), channel_id=1, source_target_pairs={{0,1},{1,0},{2,3},{3,2},{4,5},{5,4},{6,7},{7,6},{8,9},{9,8},{10,11... | collective-permute-start | bytes 1179656 | tf_op jit(solution)/shard_map/ppermute | solution.py:196
  645.5 104.0 %collective-permute-start.6 = (bf16[64,4096]{1,0:T(8,128)(2,1)}, bf16[64,4096]{1,0:T(8,128)(2,1)S(1)}, u32[]{:S(2)}, u32[]{:S(2)}) collective-permute-start(bf16[64,4096]{1,0:T(8,128)(2,1)} %reduce-scatter.9.cloned.1.call-done), channel_id=1, source_target_pairs={{0,1},{1,0},{2,3},{3,2},{4,5},{5,4},{6,7},{7,6},{8,9},{9,8},{10,11... | collective-permute-start | bytes 1572872 | tf_op jit(solution)/shard_map/ppermute | solution.py:196
  748.1 13.9 %collective-permute-start.7 = (bf16[256,1024]{1,0:T(8,128)(2,1)}, bf16[256,1024]{1,0:T(8,128)(2,1)S(1)}, u32[]{:S(2)}, u32[]{:S(2)}) collective-permute-start(bf16[256,1024]{1,0:T(8,128)(2,1)} %reduce-scatter.11.cloned.1.call-done), channel_id=1, source_target_pairs={{0,1},{1,0},{2,3},{3,2},{4,5},{5,4},{6,7},{7,6},{8,9},{9,8},{10,11... | collective-permute-start | bytes 1572872 | tf_op jit(solution)/shard_map/ppermute | solution.py:196
  (41 other events, 689.5 us)
Sparse Core Ops, SparseCore 0:
  10.3 70.8 all-gather.7
  83.3 40.2 all-gather.9
  125.8 73.7 all-gather.11
  201.6 73.1 all-gather.13
  355.3 59.9 reduce-scatter.6
  447.1 83.7 reduce-scatter.4
  535.0 104.7 reduce-scatter.8
  643.8 104.2 reduce-scatter.10

commit v2 on v1

--- a/solution.py
+++ b/solution.py
@@ -277,16 +277,20 @@
     grad_result = cot_own.astype(f32)
     grad_output = (gate_two[:, None, :] * grad_result).astype(bf16)
     grad_gate_two = jnp.sum(grad_result * output, axis=1)
-    grad_down_weight = scatter_rows(
-        jnp.einsum("btf,btd->fd", active, grad_output, preferred_element_type=f32), parts
-    )
+    partial_down = jnp.einsum(
+        "btf,btd->fd", active, grad_output, preferred_element_type=f32
+    ).astype(bf16)
+    grad_output, partial_down = lax.optimization_barrier((grad_output, partial_down))
+    grad_down_weight = scatter_rows(partial_down, parts)
     grad_down_bias = jnp.sum(grad_output, axis=(0, 1), dtype=f32)
     grad_active = jnp.einsum("btd,fd->btf", grad_output, w_down, preferred_element_type=f32)
     unused, gelu_back = jax.vjp(gelu_tanh, hidden)
     grad_hidden = gelu_back(grad_active)[0].astype(bf16)
-    grad_up_weight = scatter_rows(
-        jnp.einsum("btd,btf->df", normed_two, grad_hidden, preferred_element_type=f32), parts
-    )
+    partial_up = jnp.einsum(
+        "btd,btf->df", normed_two, grad_hidden, preferred_element_type=f32
+    ).astype(bf16)
+    grad_hidden, partial_up = lax.optimization_barrier((grad_hidden, partial_up))
+    grad_up_weight = scatter_rows(partial_up, parts)
     grad_up_bias = jnp.sum(grad_hidden, axis=(0, 1), dtype=f32)
     grad_normed_two = jnp.einsum("btf,df->btd", grad_hidden, w_up, preferred_element_type=f32)
     unused, norm_back_two = jax.vjp(modulate, middle, shift_two, scale_two)
@@ -294,13 +298,16 @@
     grad_middle = grad_middle + grad_result
     grad_branch = (gate_one[:, None, :] * grad_middle).astype(bf16)
     grad_gate_one = jnp.sum(grad_middle * branch, axis=1)
-    grad_proj_weight = scatter_rows(
-        jnp.einsum("bte,btd->ed", attended, grad_branch, preferred_element_type=f32), parts
-    )
+    partial_proj = jnp.einsum(
+        "bte,btd->ed", attended, grad_branch, preferred_element_type=f32
+    ).astype(bf16)
+    grad_branch, partial_proj = lax.optimization_barrier((grad_branch, partial_proj))
+    grad_proj_weight = scatter_rows(partial_proj, parts)
     grad_proj_bias = jnp.sum(grad_branch, axis=(0, 1), dtype=f32)
     grad_attended = jnp.einsum(
         "btd,ed->bte", grad_branch, w_proj, preferred_element_type=f32
     ).astype(bf16)
+    grad_attended, grad_down_weight = lax.optimization_barrier((grad_attended, grad_down_weight))
     grad_qkv = attend_back(qkv, grad_attended, lse)
     grad_qkv_weight = scatter_rows(
         jnp.einsum("btd,bte->de", normed_one, grad_qkv, preferred_element_type=f32), parts

time: 775 us -> 718 us (0.926)
  waiting for transfers between devices: 228 us -> 163 us
  other arithmetic: 47.7 us -> 57 us
    reduce_scatter x4, waiting for transfers between devices: 93.3 us -> 39.3 us  [scatter_rows(): lax.psum_scatter(g.astype(bf16), 'shard', scatter_dimension=0, tiled=True)]
    all_gather x4, waiting for transfers between devices: 101 us -> 82.6 us  [gather_rows(): return lax.all_gather(x, 'shard', axis=0, tiled=True)]
    ppermute x2, waiting for transfers between devices: 0.01 us -> 15.3 us  [swap_out(): lax.ppermute(x[:, rows:].astype(bf16), 'seq', [(0, 1), (1, 0)])]
  transfers between devices with their start and end apart: 19 -> 19, of which waited for: 8 -> 10; matrix products, arithmetic and copies ran while one was open for 21% -> 36% of each run, Pallas kernels for 17% -> 18%
where the time goes in v2:
time: 718 us; the launch traced here: 714 us
  waiting for transfers between devices  163 us (23%)
  matrix products  156 us (22%)
  Pallas kernels  129 us (18%)
  blocking collectives  113 us (16%)
  local copies, waits for them, and re-layouts  58.4 us (8%)
  other arithmetic  57 us (8%)
  starting transfers between devices  23.6 us (3%)
  between operations  15 us (2%)
    all_gather x1, blocking collectives, shards(): everyone = lax.all_gather(sent, ('shard', 'seq'), axis=0, tiled=False)  90.5 us
    all_gather x4, waiting for transfers between devices, gather_rows(): return lax.all_gather(x, 'shard', axis=0, tiled=True)  82.6 us
    pallas_call x1, Pallas kernels, attend_back(): pl.pallas_call(functools.partial(attend_back_kernel, chunk), grid=(latent...  75.5 us
    pallas_call x1, Pallas kernels, attend(): pl.pallas_call(functools.partial(attend_kernel, chunk), grid=(latents, pa...  53.5 us
    reduce_scatter x4, waiting for transfers between devices, scatter_rows(): lax.psum_scatter(g.astype(bf16), 'shard', scatter_dimension=0, tiled=True)  39.3 us
    unnamed x107, local copies, waits for them, and re-layouts  32.1 us
    dot_general x1, matrix products, shards(): jnp.einsum('btd,fd->btf', grad_output, w_down, preferred_element_type=f32)  26.9 us
    all_gather x1, blocking collectives, shards(): lax.all_gather(jnp.concatenate(biases), 'shard', axis=0, tiled=False)  22 us
  transfers between devices with their start and end apart: 19, of which 10 were waited for; matrix products, arithmetic and copies ran while one was open for 36% of the time, Pallas kernels for 18%

profile of v2, /device:TPU:0, one launch (start us, length us, event | category | flops | bytes accessed | tf_op | source)
XLA Modules:
  0.0 714.3 jit_solution(10630185532634689181)
XLA Ops:
  11.4 7.4 %all-to-all-start = ((bf16[16,2,64]{2,1,0:T(2,128)(2,1)}), bf16[16,2,64]{2,1,0:T(2,128)(2,1)S(1)}, u32[]{:S(2)}, u32[]{:S(2)}) async-start(bf16[16,2,64]{2,1,0:T(2,128)(2,1)} %copy.97), calls=%async_computation | async-start | bytes 16384 | tf_op jit(solution)/shard_map/all_to_all | solution.py:240
  28.1 22.0 %all-gather.2 = bf16[16,1,512]{2,1,0:T(2,128)(2,1)S(1)} all-gather(bf16[1,1,512]{2,1,0:T(2,128)(2,1)S(1)} %reshape.655), channel_id=2, replica_groups=mesh['shard'=16,'seq'=2] {'shard'}, dimensions={0}, use_global_device_ids=true | all-gather | bytes 17408 | tf_op jit(solution)/shard_map/all_gather | solution.py:232
  60.5 12.7 %all-to-all-done.1 = f32[16,1,6144]{2,1,0:T(1,128)S(1)} async-done(((f32[16,1,6144]{2,1,0:T(1,128)}), f32[16,1,6144]{2,1,0:T(1,128)S(1)}, u32[]{:S(2)}, u32[]{:S(2)}) %all-to-all-start.1) | async-done | bytes 393248 | tf_op jit(solution)/shard_map/all_to_all | solution.py:250
  81.2 10.5 %fusion.10.q_ref.k_ref.v_ref = bf16[1,1024,3072]{2,1,0:T(8,128)(2,1)S(1)} fusion(f32[3072]{0:T(1024)S(1)} %pad_maximum_fusion.3, bf16[1024,3072]{1,0:T(8,128)(2,1)} %all-gather.8.cloned.1.call-done, f32[1024]{0:T(1024)S(1)} %bitcast.140, f32[1024]{0:T(1024)S(1)} %bitcast.123, f32[1024]{0:T(1024)S(1)} %fusion.56, f32[1024]{0:T(1024)S(1)} %broadcast_multiply_fusion.1, ...), kind=kOutput, calls=%fused_computation.17 | convolution fusion | flops 6458179584 | bytes 14708736 | tf_op jit(solution)/shard_map/btd,de->bte/dot_general | solution.py:266
  91.7 53.5 %attend.1 = (bf16[1,1024,1024]{2,1,0:T(8,128)(2,1)S(1)}, f32[1,8,2,1024]{3,2,1,0:T(2,128)S(1)}) custom-call(bf16[1,1024,3072]{2,1,0:T(8,128)(2,1)S(1)} %fusion.10.q_ref.k_ref.v_ref, bf16[1,1024,3072]{2,1,0:T(8,128)(2,1)S(1)} %fusion.10.q_ref.k_ref.v_ref, bf16[1,1024,3072]{2,1,0:T(8,128)(2,1)S(1)} %fusion.10.q_ref.k_ref.v_ref), custom_call_target="tpu_custom_call" | custom-call | flops 8589934592 | bytes 9437184 | tf_op jit(solution)/shard_map/attend/pallas_call | solution.py:60
  147.9 7.9 %fusion.66 = (f32[1024]{0:T(1024)S(1)}, f32[1024,1024]{0,1:T(8,128)S(1)}, f32[1024,1024]{0,1:T(8,128)}) fusion(f32[1024]{0:T(1024)S(1)} %add.210, f32[1024]{0:T(1024)S(1)} %bitcast.136, bf16[512,1024]{0,1:T(8,128)(2,1)} %bitcast.104, bf16[512,1024]{0,1:T(8,128)(2,1)} %bitcast.98, bf16[1024,1024]{1,0:T(8,128)(2,1)} %all-gather.10.cloned.1.call-done, ...), kind=kOutput, calls=%fused_computation.131 | convolution fusion | flops 2155871232 | bytes 14692352 | tf_op jit(solution)/shard_map/bte,ed->btd/dot_general | solution.py:269
  158.3 41.4 %all-gather.12.cloned.1.call-done = bf16[1024,4096]{1,0:T(8,128)(2,1)} async-done(((bf16[64,4096]{1,0:T(8,128)(2,1)}), bf16[1024,4096]{1,0:T(8,128)(2,1)}) %all-gather.12.cloned.1.call-update) | async-done | bytes 8388624 | tf_op jit(solution)/shard_map/all_gather | solution.py:191
  199.6 20.9 %multiply_convert_fusion = (bf16[1024,4096]{1,0:T(8,128)(2,1)S(1)}, f32[1024,4096]{1,0:T(8,128)}) fusion(f32[4096]{0:T(1024)S(1)} %bitcast.138, bf16[1024,4096]{1,0:T(8,128)(2,1)} %all-gather.12.cloned.1.call-done, f32[1024,1024]{0,1:T(8,128)} %copy-done.6, f32[1024]{0:T(1024)S(1)} %bitcast.142, f32[1024]{0:T(1024)S(1)} %bitcast.131, f32[1024]{0:T(1024)S(1)} %fusion.57, ...), kind=kOutput, calls=%fused_computation.9 | convolution fusion | flops 8637120512 | bytes 37781504 | tf_op jit(solution)/shard_map/btd,df->btf/dot_general | solution.py:272
  223.8 12.9 %convolution_convert_fusion.1 = bf16[4096,1024]{1,0:T(8,128)(2,1)} fusion(bf16[1024,4096]{1,0:T(8,128)(2,1)S(1)} %get-tuple-element.144, f32[1024]{0:T(1024)S(1)} %bitcast.129, bf16[512,1024]{0,1:T(8,128)(2,1)} %bitcast.18, bf16[512,1024]{0,1:T(8,128)(2,1)S(1)} %bitcast.109), kind=kOutput, calls=%fused_computation.14 | convolution fusion | flops 8600420352 | bytes 18878464 | tf_op jit(solution)/shard_map/btf,btd->fd/dot_general | solution.py:280
  236.8 38.0 %all-gather.14.cloned.1.call-done = bf16[4096,1024]{1,0:T(8,128)(2,1)} async-done(((bf16[256,1024]{1,0:T(8,128)(2,1)}), bf16[4096,1024]{1,0:T(8,128)(2,1)}) %all-gather.14.cloned.1.call-update) | async-done | bytes 8388624 | tf_op jit(solution)/shard_map/all_gather | solution.py:191
  274.8 26.9 %fusion.6 = bf16[1024,4096]{1,0:T(8,128)(2,1)} fusion(f32[1024,4096]{1,0:T(8,128)} %get-tuple-element.145, f32[4096]{0:T(1024)S(1)} %bitcast.139, bf16[4096,1024]{1,0:T(8,128)(2,1)} %all-gather.14.cloned.1.call-done, bf16[1,1024,1024]{1,2,0:T(8,128)(2,1)} %multiply_convert_fusion.2), kind=kOutput, calls=%fused_computation.8 | convolution fusion | flops 8678014976 | bytes 35667968 | tf_op jit(solution)/shard_map/btd,fd->btf/dot_general | solution.py:286
  301.7 15.8 %convolution_convert_fusion = bf16[1024,4096]{1,0:T(8,128)(2,1)} fusion(bf16[1024,4096]{1,0:T(8,128)(2,1)} %fusion.6, f32[1024,1024]{0,1:T(8,128)} %copy-done.6, f32[1024]{0:T(1024)S(1)} %bitcast.143, f32[1024]{0:T(1024)S(1)} %bitcast.132, f32[1024]{0:T(1024)S(1)} %fusion.57, f32[1024]{0:T(1024)S(1)} %broadcast_multiply_fusion), kind=kOutput, calls=%fused_computation.13 | convolution fusion | flops 8599371776 | bytes 20987904 | tf_op jit(solution)/shard_map/btd,btf->df/dot_general | solution.py:289
  317.5 15.2 %fusion.72 = (bf16[1024]{0:T(1024)(128)(2,1)S(1)}, f32[1024,1024]{1,0:T(8,128)}) fusion(bf16[1024,4096]{1,0:T(8,128)(2,1)} %all-gather.12.cloned.1.call-done, bf16[1,1024,4096]{2,1,0:T(8,128)(2,1)} %bitcast.114), kind=kOutput, calls=%fused_computation.137 | convolution fusion | flops 8590982144 | bytes 20973568 | tf_op jit(solution)/shard_map/btf,df->btd/dot_general | solution.py:295
  347.3 15.2 %fusion.73 = f32[1024,1024]{0,1:T(8,128)} fusion(bf16[1024,4096]{1,0:T(8,128)(2,1)} %copy-done.44, bf16[4096,1024]{1,0:T(8,128)(2,1)} %all-gather.14.cloned.1.call-done), kind=kOutput, calls=%fused_computation.138 | convolution fusion | flops 8589934592 | bytes 20971520 | tf_op jit(solution)/shard_map/btf,fd->btd/dot_general | solution.py:274
  362.5 7.6 %fusion.30 = (bf16[1024]{0:T(1024)(128)(2,1)S(1)}, bf16[1024]{0:T(1024)(128)(2,1)S(1)}, bf16[1024,1024]{0,1:T(8,128)(2,1)S(1)}, bf16[1,1024,1024]{1,2,0:T(8,128)(2,1)}) fusion(f32[1024,1024]{0,1:T(8,128)} %fusion.73, f32[1024]{0:T(1024)S(1)} %copy-done.35, bf16[512,1024]{0,1:T(8,128)(2,1)} %bitcast.18, bf16[512,1024]{0,1:T(8,128)(2,1)S(1)} %bitcast.110, ...), kind=kLoop, calls=%fused_computation.44 | loop fusion | flops 17823744 | bytes 23093248 | tf_op jit(solution)/shard_map/reduce_sum | solution.py:279
  375.9 5.7 reduce-scatter.5.cloned.1.call-done
  387.1 8.5 %collective-permute-done.3 = bf16[256,1024]{1,0:T(8,128)(2,1)S(1)} collective-permute-done((bf16[256,1024]{1,0:T(8,128)(2,1)}, bf16[256,1024]{1,0:T(8,128)(2,1)S(1)}, u32[]{:S(2)}, u32[]{:S(2)}) %collective-permute-start.3) | collective-permute-done | bytes 524320 | tf_op jit(solution)/shard_map/ppermute | solution.py:196
  396.8 75.5 %attend_back.1 = bf16[1,1024,3072]{2,1,0:T(8,128)(2,1)S(1)} custom-call(bf16[1,1024,3072]{2,1,0:T(8,128)(2,1)} %copy-done.2, bf16[1,1024,3072]{2,1,0:T(8,128)(2,1)} %copy-done.2, bf16[1,1024,3072]{2,1,0:T(8,128)(2,1)} %copy-done.2, bf16[1,1024,1024]{2,1,0:T(8,128)(2,1)S(1)} %convert_bitcast_fusion.do_ref, f32[1,8,2,1024]{3,2,1,0:T(2,128)S(1)} %get-tuple-element.29.lse_ref), custom_call_target="tpu_custom_call" | custom-call | flops 21474836480 | bytes 12582912 | tf_op jit(solution)/shard_map/attend_back/pallas_call | solution.py:127
  475.0 9.0 %fusion.15 = bf16[1024,3072]{1,0:T(8,128)(2,1)} fusion(bf16[1,1024,3072]{2,1,0:T(8,128)(2,1)S(1)} %attend_back.1, f32[1024]{0:T(1024)S(1)} %bitcast.141, f32[1024]{0:T(1024)S(1)} %bitcast.124, f32[1024]{0:T(1024)S(1)} %copy-done.32, f32[1024]{0:T(1024)S(1)} %copy-done.26, bf16[512,1024]{0,1:T(8,128)(2,1)S(1)} %bitcast.105, bf16[512,1024]{0,1:T(8,128)(2,1)S(1)} %bitcast.99), kind=kOutput, calls=%fused_computation.27 | convolution fusion | flops 6455033856 | bytes 14696448 | tf_op jit(solution)/shard_map/btd,bte->de/dot_general | solution.py:313
  497.8 15.3 %collective-permute-done.1 = bf16[1,512,1024]{1,2,0:T(8,128)(2,1)} collective-permute-done((bf16[1,512,1024]{1,2,0:T(8,128)(2,1)}, bf16[1,512,1024]{1,2,0:T(8,128)(2,1)}, u32[]{:S(2)}, u32[]{:S(2)}) %collective-permute-start.1) | collective-permute-done | bytes 1048608 | tf_op jit(solution)/shard_map/ppermute | solution.py:184
  521.7 33.6 %reduce-scatter.11.cloned.1.call-done = bf16[64,4096]{1,0:T(8,128)(2,1)} async-done(((bf16[1024,4096]{1,0:T(8,128)(2,1)}), bf16[64,4096]{1,0:T(8,128)(2,1)}) %reduce-scatter.11.cloned.1.call-update) | async-done | bytes 524304 | tf_op jit(solution)/shard_map/reduce_scatter | solution.py:201
  560.4 12.0 %fusion.71 = (bf16[1024]{0:T(1024)(128)(2,1)S(1)}, f32[1024,1024]{1,0:T(8,128)}) fusion(bf16[1024,3072]{1,0:T(8,128)(2,1)} %all-gather.8.cloned.1.call-done, bf16[1,1024,3072]{2,1,0:T(8,128)(2,1)} %copy-done.1), kind=kOutput, calls=%fused_computation.136 | convolution fusion | flops 6443498496 | bytes 16779264 | tf_op jit(solution)/shard_map/bte,de->btd/dot_general | solution.py:317
  572.4 5.8 copy.104
  591.8 90.5 %all-gather.1 = bf16[458752]{0:T(1024)(128)(2,1)S(1)} all-gather(bf16[14336]{0:T(1024)(128)(2,1)S(1)} %constant_dynamic-update-slice_fusion), channel_id=3, replica_groups=mesh['shard'=16,'seq'=2] {'shard','seq'}, dimensions={0}, use_global_device_ids=true | all-gather | bytes 946176 | tf_op jit(solution)/shard_map/all_gather | solution.py:342
  (225 shorter events, 135.5 us)
Async XLA Ops:
  7.2 74.0 %all-gather.8.cloned.1.call-start = ((), (), s32[]{:S(2)}) async-start(), calls=%async_computation.7 | async-start | bytes 6684672 | tf_op jit(solution)/shard_map/all_gather | solution.py:191
  7.9 140.0 %all-gather.10.cloned.1.call-start = ((), (), s32[]{:S(2)}) async-start(), calls=%async_computation.8 | async-start | bytes 2228224 | tf_op jit(solution)/shard_map/all_gather | solution.py:191
  8.7 191.0 %all-gather.12.cloned.1.call-start = ((), (), s32[]{:S(2)}) async-start(), calls=%async_computation.9 | async-start | bytes 8912896 | tf_op jit(solution)/shard_map/all_gather | solution.py:191
  9.4 265.4 %all-gather.14.cloned.1.call-start = ((), (), s32[]{:S(2)}) async-start(), calls=%async_computation.10 | async-start | bytes 8912896 | tf_op jit(solution)/shard_map/all_gather | solution.py:191
  11.4 38.7 %all-to-all-start = ((bf16[16,2,64]{2,1,0:T(2,128)(2,1)}), bf16[16,2,64]{2,1,0:T(2,128)(2,1)S(1)}, u32[]{:S(2)}, u32[]{:S(2)}) async-start(bf16[16,2,64]{2,1,0:T(2,128)(2,1)} %copy.97), calls=%async_computation | async-start | bytes 16384 | tf_op jit(solution)/shard_map/all_to_all | solution.py:240
  24.5 48.9 %collective-permute-start = (bf16[1,512,1024]{1,2,0:T(8,128)(2,1)}, bf16[1,512,1024]{1,2,0:T(8,128)(2,1)S(1)}, u32[]{:S(2)}, u32[]{:S(2)}) collective-permute-start(bf16[1,512,1024]{1,2,0:T(8,128)(2,1)} %copy.114), channel_id=1, source_target_pairs={{0,1},{1,0},{2,3},{3,2},{4,5},{5,4},{6,7},{7,6},{8,9},{9,8},{10,11... | collective-permute-start | bytes 3145736 | tf_op jit(solution)/shard_map/ppermute | solution.py:172
  27.2 47.2 %collective-permute-start.2 = (bf16[1,512,1024]{1,2,0:T(8,128)(2,1)}, bf16[1,512,1024]{1,2,0:T(8,128)(2,1)}, u32[]{:S(2)}, u32[]{:S(2)}) collective-permute-start(bf16[1,512,1024]{1,2,0:T(8,128)(2,1)} %copy.117), channel_id=1, source_target_pairs={{0,1},{1,0},{2,3},{3,2},{4,5},{5,4},{6,7},{7,6},{8,9},{9,8},{10,11... | collective-permute-start | bytes 3145736 | tf_op jit(solution)/shard_map/ppermute | solution.py:172
  51.5 21.6 %all-to-all-start.1 = ((f32[16,1,6144]{2,1,0:T(1,128)}), f32[16,1,6144]{2,1,0:T(1,128)S(1)}, u32[]{:S(2)}, u32[]{:S(2)}) async-start(f32[16,1,6144]{2,1,0:T(1,128)} %copy.99), calls=%async_computation.1 | async-start | bytes 786432 | tf_op jit(solution)/shard_map/all_to_all | solution.py:250
  55.1 326.6 %reduce-scatter.5.cloned.1.call-start = ((), (), s32[]{:S(2)}) async-start(), calls=%async_computation.11 | async-start | bytes 8912896 | tf_op jit(solution)/shard_map/reduce_scatter | solution.py:201
  236.8 260.5 %reduce-scatter.9.cloned.1.call-start = ((), (), s32[]{:S(2)}) async-start(), calls=%async_computation.13 | async-start | bytes 2228224 | tf_op jit(solution)/shard_map/reduce_scatter | solution.py:201
  375.1 180.1 %reduce-scatter.11.cloned.1.call-start = ((), (), s32[]{:S(2)}) async-start(), calls=%async_computation.14 | async-start | bytes 8912896 | tf_op jit(solution)/shard_map/reduce_scatter | solution.py:201
  375.9 319.0 %reduce-scatter.7.cloned.1.call-start = ((), (), s32[]{:S(2)}) async-start(), calls=%async_computation.12 | async-start | bytes 6684672 | tf_op jit(solution)/shard_map/reduce_scatter | solution.py:201
  381.6 13.9 %collective-permute-start.3 = (bf16[256,1024]{1,0:T(8,128)(2,1)}, bf16[256,1024]{1,0:T(8,128)(2,1)S(1)}, u32[]{:S(2)}, u32[]{:S(2)}) collective-permute-start(bf16[256,1024]{1,0:T(8,128)(2,1)} %reduce-scatter.5.cloned.1.call-done), channel_id=1, source_target_pairs={{0,1},{1,0},{2,3},{3,2},{4,5},{5,4},{6,7},{7,6},{8,9},{9,8},{10,11... | collective-permute-start | bytes 1572872 | tf_op jit(solution)/shard_map/ppermute | solution.py:196
  396.7 78.2 %copy-start.26 = (f32[1024]{0:T(1024)S(1)}, f32[1024]{0:T(1024)}, u32[]{:S(2)}) copy-start(f32[1024]{0:T(1024)} %copy-done.25) | copy-start | bytes 12292
  396.7 78.2 %copy-start.30 = (f32[1,1024]{1,0:T(1,128)S(1)}, f32[1,1024]{1,0:T(1,128)}, u32[]{:S(2)}) copy-start(f32[1,1024]{1,0:T(1,128)} %copy-done.29) | copy-start | bytes 12292
  396.7 78.2 %copy-start.32 = (f32[1024]{0:T(1024)S(1)}, f32[1024]{0:T(1024)}, u32[]{:S(2)}) copy-start(f32[1024]{0:T(1024)} %copy-done.31) | copy-start | bytes 12292
  487.1 26.0 %collective-permute-start.1 = (bf16[1,512,1024]{1,2,0:T(8,128)(2,1)}, bf16[1,512,1024]{1,2,0:T(8,128)(2,1)}, u32[]{:S(2)}, u32[]{:S(2)}) collective-permute-start(bf16[1,512,1024]{1,2,0:T(8,128)(2,1)} %get-tuple-element.126), channel_id=1, source_target_pairs={{0,1},{1,0},{2,3},{3,2},{4,5},{5,4},{6,7},{7,6},{8,9},{9,8},{10,11... | collective-permute-start | bytes 3145736 | tf_op jit(solution)/shard_map/ppermute | solution.py:184
  497.3 23.7 %collective-permute-start.6 = (bf16[64,1024]{1,0:T(8,128)(2,1)}, bf16[64,1024]{1,0:T(8,128)(2,1)S(1)}, u32[]{:S(2)}, u32[]{:S(2)}) collective-permute-start(bf16[64,1024]{1,0:T(8,128)(2,1)} %reduce-scatter.9.cloned.1.call-done), channel_id=1, source_target_pairs={{0,1},{1,0},{2,3},{3,2},{4,5},{5,4},{6,7},{7,6},{8,9},{9,8},{10,11... | collective-permute-start | bytes 393224 | tf_op jit(solution)/shard_map/ppermute | solution.py:196
  555.3 132.0 %collective-permute-start.7 = (bf16[64,4096]{1,0:T(8,128)(2,1)}, bf16[64,4096]{1,0:T(8,128)(2,1)}, u32[]{:S(2)}, u32[]{:S(2)}) collective-permute-start(bf16[64,4096]{1,0:T(8,128)(2,1)} %reduce-scatter.11.cloned.1.call-done), channel_id=1, source_target_pairs={{0,1},{1,0},{2,3},{3,2},{4,5},{5,4},{6,7},{7,6},{8,9},{9,8},{10,11... | collective-permute-start | bytes 1572872 | tf_op jit(solution)/shard_map/ppermute | solution.py:196
  589.7 97.5 %copy-start.21 = (bf16[64,4096]{1,0:T(8,128)(2,1)S(1)}, bf16[64,4096]{1,0:T(8,128)(2,1)}, u32[]{:S(2)}) copy-start(bf16[64,4096]{1,0:T(8,128)(2,1)} %reduce-scatter.11.cloned.1.call-done) | copy-start | bytes 1572868
  589.7 99.7 %copy-start.28 = (bf16[16,2,64]{2,1,0:T(2,128)(2,1)S(1)}, bf16[16,2,64]{2,1,0:T(2,128)(2,1)}, u32[]{:S(2)}) copy-start(bf16[16,2,64]{2,1,0:T(2,128)(2,1)} %copy-done.27) | copy-start | bytes 12292
  590.9 105.2 %collective-permute-start.4 = (bf16[1,512,1024]{1,2,0:T(8,128)(2,1)}, bf16[1,512,1024]{1,2,0:T(8,128)(2,1)}, u32[]{:S(2)}, u32[]{:S(2)}) collective-permute-start(bf16[1,512,1024]{1,2,0:T(8,128)(2,1)} %slice.122), channel_id=1, source_target_pairs={{0,1},{1,0},{2,3},{3,2},{4,5},{5,4},{6,7},{7,6},{8,9},{9,8},{10,11... | collective-permute-start | bytes 3145736 | tf_op jit(solution)/shard_map/ppermute | solution.py:184
  683.7 9.8 %all-to-all-start.2 = ((f32[16,1,128]{2,1,0:T(1,128)}), f32[16,1,128]{2,1,0:T(1,128)S(1)}, u32[]{:S(2)}, u32[]{:S(2)}) async-start(f32[16,1,128]{2,1,0:T(1,128)} %bitcast.29), calls=%async_computation.3 | async-start | bytes 16384 | tf_op jit(solution)/shard_map/all_to_all | solution.py:362
  694.9 11.4 %collective-permute-start.5 = (bf16[64,3072]{1,0:T(8,128)(2,1)}, bf16[64,3072]{1,0:T(8,128)(2,1)S(1)}, u32[]{:S(2)}, u32[]{:S(2)}) collective-permute-start(bf16[64,3072]{1,0:T(8,128)(2,1)} %reduce-scatter.7.cloned.1.call-done), channel_id=1, source_target_pairs={{0,1},{1,0},{2,3},{3,2},{4,5},{5,4},{6,7},{7,6},{8,9},{9,8},{10,11... | collective-permute-start | bytes 1179656 | tf_op jit(solution)/shard_map/ppermute | solution.py:196
  (42 other events, 525.5 us)
Sparse Core Ops, SparseCore 0:
  10.3 70.7 all-gather.7
  83.3 40.6 all-gather.9
  126.2 73.4 all-gather.11
  201.7 73.1 all-gather.13
  278.8 102.8 reduce-scatter.4
  385.2 61.7 reduce-scatter.8
  451.6 103.5 reduce-scatter.10
  559.7 86.4 reduce-scatter.6
